TPU v7x, 256 devices: a whole 4x4x8 slice. The times are simulated.
256 devices in a mesh: section: 8 (over z), row: 4 (over x_lo, core), col: 8 (over x_hi, y).
Axes of the slice: x: 4 (x_hi: 2, x_lo: 2; x = x_hi * 2 + x_lo), y: 4, z: 8, core: 2. Of those that a mesh axis runs over, the one named last changes fastest.
Arguments:
- layer_input: bfloat16 [8, 256, 6144], P('section', ('row', 'col')), may hold values from -6 to 6
- output_grad: bfloat16 [8, 256, 6144], P('section', ('row', 'col')), may hold values from -6 to 6
- up_panels: bfloat16 [8, 1536, 24576], P('section', 'row', 'col'), may hold values from -0.15625 to 0.15625
- up_rows: int32 [8, 12, 192], P('section', 'row', 'col'), may hold values from 0 to 11, as said below
- up_counts: int32 [8, 4, 192], P('section', 'row', 'col'), may hold values from 0 to 3, as said below
- down_panels: bfloat16 [8, 6144, 6144], P('section', 'col', 'row'), may hold values from -0.15625 to 0.15625
- down_rows: int32 [8, 48, 48], P('section', 'col', 'row'), may hold values from 0 to 23, as said below
- down_counts: int32 [8, 8, 48], P('section', 'col', 'row'), may hold values from 0 to 6, as said below
Outputs:
- received: bfloat16 [8, 256, 6144], P('section', ('row', 'col'))
- up_grad: bfloat16 [8, 1536, 24576], P('section', 'row', 'col')
- down_grad: bfloat16 [8, 6144, 6144], P('section', 'col', 'row')
Inputs may be any that keep to these rules, and one draw needn't show every extreme that they name: For every section, tile row r and column block j, the 3 entries up_rows[s, r * 3 + k, j] are distinct. `up_counts`: in every section and tile row some column block has all 3 slots live; counts differ from column to column. For every section, tile column c and feature block j, the 6 entries down_rows[s, c * 6 + k, j] are distinct. `down_counts`: in every section and tile column some feature block has all 6 slots live; counts differ from block to block.
All inputs are finite; a program needn't handle non-finite values.
Results may differ from a plain program's by a relative error of at most 0.022.
Values may be sent and summed in bfloat16 or wider, within the bound.
A program may use at most 128 MiB of HBM per device.

v0:
```python
import math

import jax
import jax.numpy as jnp
from jax import lax
from jax.sharding import PartitionSpec as P

BLK = 128


TANH_SCALE = math.sqrt(2.0 / math.pi)
CUBIC = 0.044715


def shifted(block, axis, distance):
    devices = range(lax.axis_size(axis))
    route = [(i - distance, i) for i in devices if i - distance in devices]
    return lax.ppermute(block, axis, route)


def gelu_value(value):
    inner = TANH_SCALE * (value + CUBIC * value * value * value)
    return 0.5 * value * (1.0 + jnp.tanh(inner))


def gelu_slope(value):
    inner = TANH_SCALE * (value + CUBIC * value * value * value)
    tangent = jnp.tanh(inner)
    return 0.5 * (1.0 + tangent) + 0.5 * value * (1.0 - tangent * tangent) * TANH_SCALE * (
        1.0 + 3.0 * CUBIC * value * value
    )


def shards(
    layer_input, output_grad, up_panels, up_rows, up_counts, down_panels, down_rows, down_counts
):
    row_count = lax.axis_size("row")
    col_count = lax.axis_size("col")
    own_input = layer_input[0]
    own_grad = output_grad[0]
    share_rows = own_input.shape[0]
    width_all = own_input.shape[1]
    all_tokens = share_rows * row_count * col_count
    tile_width = width_all // row_count
    row_blocks = tile_width // BLK
    gathered = (
        lax.all_gather(own_input, ("row", "col"), axis=0, tiled=True),
        lax.all_gather(own_grad, ("row", "col"), axis=0, tiled=True),
    )
    offset = lax.axis_index("row") * tile_width
    input_rows = lax.dynamic_slice_in_dim(gathered[0], offset, tile_width, 1)
    grad_rows = lax.dynamic_slice_in_dim(gathered[1], offset, tile_width, 1)
    up_slots = up_rows.shape[1]
    up_cols = up_rows.shape[2]
    hidden_width = up_cols * BLK
    up_view = up_panels[0].reshape(up_slots, BLK, up_cols, BLK)
    up_live = jnp.arange(up_slots, dtype=jnp.int32)[:, None] < up_counts[0]
    up_masked = jnp.where(up_live[:, None, :, None], up_view, jnp.zeros((), jnp.bfloat16))
    up_targets = up_rows[0]
    selected = jnp.take(input_rows.reshape(all_tokens, row_blocks, BLK), up_targets, axis=1)
    down_slots = down_rows.shape[1]
    down_view = down_panels[0].reshape(down_slots, BLK, row_blocks, BLK)
    down_live = jnp.arange(down_slots, dtype=jnp.int32)[:, None] < down_counts[0]
    down_masked = jnp.where(down_live[:, None, :, None], down_view, jnp.zeros((), jnp.bfloat16))
    down_targets = down_rows[0]
    grad_blocks = grad_rows.reshape(all_tokens, row_blocks, BLK)
    share_count = all_tokens // row_count
    picked = selected
    product = jnp.einsum("tkjp,kpjq->tjq", picked, up_masked, preferred_element_type=jnp.float32)
    hidden_share = lax.psum_scatter(
        product.reshape(share_count * lax.axis_size("row"), hidden_width).astype(jnp.bfloat16),
        "row",
        scatter_dimension=0,
        tiled=True,
    ).astype(jnp.float32)
    picked = grad_blocks
    spread = jnp.einsum("tjq,kpjq->tkjp", picked, down_masked, preferred_element_type=jnp.float32)
    placed = (
        jnp.zeros((share_count * lax.axis_size("row"), up_cols, BLK), jnp.float32)
        .at[:, down_targets]
        .add(spread)
    )
    act_grad_share = lax.psum_scatter(
        placed.reshape(share_count * lax.axis_size("row"), hidden_width).astype(jnp.bfloat16),
        "row",
        scatter_dimension=0,
        tiled=True,
    ).astype(jnp.float32)
    act_share = gelu_value(hidden_share).astype(jnp.bfloat16)
    slope_share = (act_grad_share * gelu_slope(hidden_share)).astype(jnp.bfloat16)
    activation, hidden_grad = (
        lax.all_gather(act_share, "row", axis=0, tiled=True),
        lax.all_gather(slope_share, "row", axis=0, tiled=True),
    )
    down_picked = jnp.take(activation.reshape(all_tokens, up_cols, BLK), down_targets, axis=1)
    down_product = jnp.einsum(
        "tkjp,tjq->kpjq", down_picked, grad_blocks, preferred_element_type=jnp.float32
    )
    down_grad = jnp.where(down_live[:, None, :, None], down_product, jnp.zeros((), jnp.float32))
    down_grad = down_grad.astype(jnp.bfloat16).reshape(down_slots * BLK, tile_width)
    hidden_blocks = hidden_grad.reshape(all_tokens, up_cols, BLK)
    up_product = jnp.einsum(
        "tkjp,tjq->kpjq", selected, hidden_blocks, preferred_element_type=jnp.float32
    )
    up_grad = jnp.where(up_live[:, None, :, None], up_product, jnp.zeros((), jnp.float32))
    up_grad = up_grad.astype(jnp.bfloat16).reshape(up_slots * BLK, hidden_width)
    feature_offset = lax.axis_index("row") * tile_width
    padded = jnp.zeros((share_rows * lax.axis_size(("row", "col")), width_all), jnp.float32)
    spread = jnp.einsum(
        "tjq,kpjq->tkjp", hidden_blocks, up_masked, preferred_element_type=jnp.float32
    )
    placed = (
        jnp.zeros((hidden_blocks.shape[0], row_blocks, BLK), jnp.float32)
        .at[:, up_targets]
        .add(spread)
    )
    summed = lax.psum_scatter(
        lax.dynamic_update_slice_in_dim(
            padded, placed.reshape(hidden_blocks.shape[0], tile_width), feature_offset, 1
        ).astype(jnp.bfloat16),
        ("row", "col"),
        scatter_dimension=0,
        tiled=True,
    ).astype(jnp.float32)
    input_grad = (own_grad.astype(jnp.float32) + summed).astype(jnp.bfloat16)
    received = shifted(input_grad, "section", -1)
    return (received[None], up_grad[None], down_grad[None])


def solution(mesh):
    in_specs = (
        P("section", ("row", "col"), None),
        P("section", ("row", "col"), None),
        P("section", "row", "col"),
        P("section", "row", "col"),
        P("section", "row", "col"),
        P("section", "col", "row"),
        P("section", "col", "row"),
        P("section", "col", "row"),
    )
    out_specs = (
        P("section", ("row", "col"), None),
        P("section", "row", "col"),
        P("section", "col", "row"),
    )
    return jax.shard_map(shards, mesh=mesh, in_specs=in_specs, out_specs=out_specs, check_vma=False)
```

profile of v0, /device:TPU:1, one launch (start us, length us, event | category | flops | bytes accessed | tf_op | source)
XLA Modules:
  0.0 532.7 jit_solution(17036384841882739727)
XLA Ops:
  11.8 2.9 copy.99
  14.7 87.0 %all-gather.11.cloned.1.call-done = bf16[1,256,6144]{2,1,0:T(8,128)(2,1)} async-done(((bf16[1,8,6144]{2,1,0:T(8,128)(2,1)}), bf16[1,256,6144]{2,1,0:T(8,128)(2,1)}) %all-gather.11.cloned.1.call-update) | async-done | bytes 3145744 | tf_op jit(solution)/shard_map/all_gather | solution.py:48
  101.7 90.4 %all-gather.13.cloned.1.call-done = bf16[1,256,6144]{2,1,0:T(8,128)(2,1)} async-done(((bf16[1,8,6144]{2,1,0:T(8,128)(2,1)}), bf16[1,256,6144]{2,1,0:T(8,128)(2,1)}) %all-gather.13.cloned.1.call-update) | async-done | bytes 3145744 | tf_op jit(solution)/shard_map/all_gather | solution.py:47
  195.1 5.5 %gather_fusion = bf16[72,256,128]{2,1,0:T(8,128)(2,1)} fusion(bf16[256,12,128]{2,0,1:T(8,128)(2,1)S(1)} %copy.108, s32[1024]{0:T(1024)S(1)} %pad_clamp_fusion.1), kind=kCustom, calls=%fused_computation | custom fusion | bytes 9437472 | tf_op jit(solution)/shard_map/jit(_take)/gather | solution.py:60
  200.7 5.2 bitcast_convert_fusion
  205.9 2.6 copy.136
  208.6 4.2 reshape_squeeze.7
  212.8 3.3 copy.100
  217.7 7.7 %convolution_bitcast_fusion = f32[6,12,256,128]{2,3,0,1:T(8,128)} fusion(bf16[256,12,128,1]{0,2,3,1:T(8,128)(2,1)S(1)} %bitcast.94, bf16[6,128,12,128]{1,3,0,2:T(8,128)(2,1)} %copy.100, pred[6,12]{0,1:T(8,128)(4,1)S(1)} %iota_compare_fusion.1), kind=kOutput, calls=%fused_computation.16 | convolution fusion | flops 605159424 | bytes 12582984 | tf_op jit(solution)/shard_map/tjq,kpjq->tkjp/dot_general | solution.py:77
  225.5 9.6 %copy.104 = f32[6,12,256,128]{3,2,1,0:T(8,128)} copy(f32[6,12,256,128]{2,3,0,1:T(8,128)} %convolution_bitcast_fusion) | data formatting | bytes 18874368 | tf_op jit(solution)/shard_map/tjq,kpjq->tkjp/transpose | solution.py:77
  235.4 15.1 %scatter_fusion = f32[256,24,128]{2,0,1:T(8,128)S(1)} fusion(f32[256,24,128]{2,0,1:T(8,128)S(1)} %broadcast_in_dim.88, s32[72]{0:T(128)S(1)} %reshape.158, f32[72,256,128]{2,1,0:T(8,128)} %bitcast.83), kind=kCustom, calls=%fused_computation.2 | custom fusion | flops 2359296 | bytes 28311840 | tf_op jit(solution)/shard_map/scatter-add | solution.py:81
  255.5 27.3 %reduce-scatter.10.cloned.1.call-done = bf16[64,3072]{1,0:T(8,128)(2,1)} async-done(((bf16[256,3072]{1,0:T(8,128)(2,1)}), bf16[64,3072]{1,0:T(8,128)(2,1)}) %reduce-scatter.10.cloned.1.call-update) | async-done | bytes 393232 | tf_op jit(solution)/shard_map/reduce_scatter | solution.py:83
  282.8 2.6 fusion.26
  286.2 27.9 %all-gather.7.cloned.1.call-done = bf16[256,3072]{1,0:T(8,128)(2,1)} async-done(((bf16[64,3072]{1,0:T(8,128)(2,1)}), bf16[256,3072]{1,0:T(8,128)(2,1)}) %all-gather.7.cloned.1.call-update) | async-done | bytes 1572880 | tf_op jit(solution)/shard_map/all_gather | solution.py:93
  316.6 7.2 %convolution_bitcast_fusion.1 = f32[3,24,256,128]{2,3,0,1:T(8,128)} fusion(bf16[256,24,128,1]{0,2,3,1:T(8,128)(2,1)} %bitcast.88, bf16[3,128,24,128]{1,3,0,2:T(8,128)(2,1)S(1)} %copy-done.2, pred[3,24]{0,1:T(8,128)(4,1)S(1)} %iota_compare_fusion), kind=kOutput, calls=%fused_computation.17 | convolution fusion | flops 605159424 | bytes 13369416 | tf_op jit(solution)/shard_map/tjq,kpjq->tkjp/dot_general | solution.py:109
  323.8 9.6 %copy.114 = f32[3,24,256,128]{3,2,1,0:T(8,128)} copy(f32[3,24,256,128]{2,3,0,1:T(8,128)} %convolution_bitcast_fusion.1) | data formatting | bytes 18874368 | tf_op jit(solution)/shard_map/tjq,kpjq->tkjp/transpose | solution.py:109
  333.6 15.1 %scatter_fusion.1 = f32[256,12,128]{2,0,1:T(8,128)S(1)} fusion(f32[256,12,128]{2,0,1:T(8,128)S(1)} %broadcast_in_dim.85, s32[72]{0:T(128)S(1)} %reshape.166, f32[72,256,128]{2,1,0:T(8,128)} %bitcast.82), kind=kCustom, calls=%fused_computation.3 | custom fusion | flops 2359296 | bytes 28311840 | tf_op jit(solution)/shard_map/scatter-add | solution.py:115
  355.7 5.4 %gather_fusion.1 = bf16[72,256,128]{2,1,0:T(8,128)(2,1)} fusion(bf16[256,24,128]{2,0,1:T(8,128)(2,1)S(1)} %copy.120, s32[1024]{0:T(1024)S(1)} %pad_clamp_fusion), kind=kCustom, calls=%fused_computation.1 | custom fusion | bytes 9437472 | tf_op jit(solution)/shard_map/jit(_take)/gather | solution.py:95
  361.1 5.3 fusion.1
  366.4 139.1 %reduce-scatter.8.cloned.1.call-done = bf16[8,6144]{1,0:T(8,128)(2,1)} async-done(((bf16[256,6144]{1,0:T(8,128)(2,1)}), bf16[8,6144]{1,0:T(8,128)(2,1)}) %reduce-scatter.8.cloned.1.call-update) | async-done | bytes 98320 | tf_op jit(solution)/shard_map/reduce_scatter | solution.py:117
  507.7 5.3 fusion
  513.0 3.1 copy.118
  518.6 3.8 copy.122
  522.3 2.9 broadcast_in_dim_reshape.7
  (72 shorter events, 30.2 us)
Async XLA Ops:
  7.2 94.5 %all-gather.11.cloned.1.call-start = ((), (), s32[]{:S(2)}) async-start(), calls=%async_computation.6 | async-start | bytes 3244032 | tf_op jit(solution)/shard_map/all_gather | solution.py:48
  7.9 184.2 %all-gather.13.cloned.1.call-start = ((), (), s32[]{:S(2)}) async-start(), calls=%async_computation.7 | async-start | bytes 3244032 | tf_op jit(solution)/shard_map/all_gather | solution.py:47
  8.6 246.8 %reduce-scatter.12.cloned.1.call-start = ((), (), s32[]{:S(2)}) async-start(), calls=%async_computation.9 | async-start | bytes 1966080 | tf_op jit(solution)/shard_map/reduce_scatter | solution.py:70
  11.7 2.9 copy-start.9
  11.7 2.9 copy-start.10
  195.1 5.6 %copy-start.1 = (bf16[3,128,24,128]{1,3,0,2:T(8,128)(2,1)S(1)}, bf16[3,128,24,128]{1,3,0,2:T(8,128)(2,1)}, u32[]{:S(2)}) copy-start(bf16[3,128,24,128]{1,3,0,2:T(8,128)(2,1)} %copy.99) | copy-start | bytes 7077892
  208.6 74.2 %reduce-scatter.10.cloned.1.call-start = ((), (), s32[]{:S(2)}) async-start(), calls=%async_computation.8 | async-start | bytes 1966080 | tf_op jit(solution)/shard_map/reduce_scatter | solution.py:83
  212.8 3.3 copy-start.8
  212.8 3.4 copy-start.11
  217.7 7.7 %copy-start.5 = (bf16[1,256,1536]{1,2,0:T(8,128)(2,1)}, bf16[1,256,1536]{1,2,0:T(8,128)(2,1)S(1)}, u32[]{:S(2)}) copy-start(bf16[1,256,1536]{1,2,0:T(8,128)(2,1)S(1)} %copy.140) | copy-start | bytes 2359300
  255.4 61.3 %copy-start.2 = (bf16[3,128,24,128]{1,3,0,2:T(8,128)(2,1)S(1)}, bf16[3,128,24,128]{1,3,0,2:T(8,128)(2,1)}, u32[]{:S(2)}) copy-start(bf16[3,128,24,128]{1,3,0,2:T(8,128)(2,1)} %copy.99) | copy-start | bytes 7077892
  255.4 58.7 %all-gather.7.cloned.1.call-start = ((), (), s32[]{:S(2)}) async-start(), calls=%async_computation.3 | async-start | bytes 1966080 | tf_op jit(solution)/shard_map/all_gather | solution.py:93
  285.4 67.6 %all-gather.9.cloned.1.call-start = ((), (), s32[]{:S(2)}) async-start(), calls=%async_computation.5 | async-start | bytes 1966080 | tf_op jit(solution)/shard_map/all_gather | solution.py:92
  286.0 219.5 %reduce-scatter.8.cloned.1.call-start = ((), (), s32[]{:S(2)}) async-start(), calls=%async_computation.4 | async-start | bytes 3244032 | tf_op jit(solution)/shard_map/reduce_scatter | solution.py:117
  350.1 1.1 copy-start.4
  351.3 1.6 copy-start
  355.7 5.5 %copy-start.3 = (bf16[256,3072]{0,1:T(8,128)(2,1)S(1)}, bf16[256,3072]{0,1:T(8,128)(2,1)}, u32[]{:S(2)}) copy-start(bf16[256,3072]{0,1:T(8,128)(2,1)} %copy.111) | copy-start | bytes 4718596
  361.1 144.4 %copy-start.7 = (bf16[1,8,6144]{2,1,0:T(8,128)(2,1)S(1)}, bf16[1,8,6144]{2,1,0:T(8,128)(2,1)}, u32[]{:S(2)}) copy-start(bf16[1,8,6144]{2,1,0:T(8,128)(2,1)} %param.9) | copy-start | bytes 294916
  361.1 146.6 %copy-start.6 = (bf16[1,256,1536]{1,2,0:T(8,128)(2,1)S(1)}, bf16[1,256,1536]{1,2,0:T(8,128)(2,1)}, u32[]{:S(2)}) copy-start(bf16[1,256,1536]{1,2,0:T(8,128)(2,1)} %copy-done.5) | copy-start | bytes 2359300
  506.4 18.8 %collective-permute-start = (bf16[8,6144]{1,0:T(8,128)(2,1)S(1)}, bf16[8,6144]{1,0:T(8,128)(2,1)S(1)}, u32[]{:S(2)}, u32[]{:S(2)}) collective-permute-start(bf16[8,6144]{1,0:T(8,128)(2,1)S(1)} %fusion.30), channel_id=1, source_target_pairs={{32,0},{64,32},{96,64},{128,96},{160,128},{192,160},{224,192},{33,... | collective-permute-start | bytes 294920 | tf_op jit(solution)/shard_map/ppermute | solution.py:18
Sparse Core Ops, SparseCore 0:
  9.8 91.8 all-gather.10
  103.5 88.5 all-gather.12
  208.7 27.2 reduce-scatter.11
  255.5 27.2 reduce-scatter.9
  285.5 28.4 all-gather.6
  315.7 28.2 all-gather.8
  353.1 152.3 reduce-scatter.7
where the time goes:
time: 539 us; the launch traced here: 533 us
  waiting for transfers between devices  374 us (69%)
  local copies, waits for them, and re-layouts  76.2 us (14%)
  other arithmetic  35.9 us (7%)
  matrix products  30.7 us (6%)
  between operations  14.4 us (3%)
    reduce_scatter x1, waiting for transfers between devices, shards(): lax.psum_scatter(lax.dynamic_update_slice_in_dim(padded, placed.reshape(h...  139 us
    all_gather x1, waiting for transfers between devices, shards(): lax.all_gather(own_input, ('row', 'col'), axis=0, tiled=True)  90.4 us
    all_gather x1, waiting for transfers between devices, shards(): lax.all_gather(own_grad, ('row', 'col'), axis=0, tiled=True)  87 us
    all_gather x1, waiting for transfers between devices, shards(): lax.all_gather(slope_share, 'row', axis=0, tiled=True)  27.9 us
    reduce_scatter x1, waiting for transfers between devices, shards(): lax.psum_scatter(placed.reshape(share_count * lax.axis_size('row'), hidde...  27.3 us
    scatter-add x1, other arithmetic, shards(): placed = jnp.zeros((hidden_blocks.shape[0], row_blocks, BLK), jnp.float32...  15.1 us
    scatter-add x1, other arithmetic, shards(): placed = jnp.zeros((share_count * lax.axis_size('row'), up_cols, BLK), jn...  15.1 us
    unnamed x30, local copies, waits for them, and re-layouts  11.4 us
  transfers between devices with their start and end apart: 8, of which 5 were waited for; matrix products, arithmetic and copies ran while one was open for 22% of the time, Pallas kernels for 0%

commit v1 on v0

v1 whole, which is shorter than its diff:
```python
import functools
import math

import jax
import jax.numpy as jnp
from jax import lax
from jax.experimental import pallas as pl
from jax.experimental.pallas import tpu as pltpu
from jax.sharding import PartitionSpec as P

BLK = 128
TANH_SCALE = math.sqrt(2.0 / math.pi)
CUBIC = 0.044715
MESH = pl.DeviceIdType.MESH
F32 = jnp.float32
BF16 = jnp.bfloat16

TOK = 256
SHARE = 8
TW = 1536
HW = 3072
HH = HW // 2
D = 4 * TW
RB = TW // BLK
CB = HW // BLK
KU = 3
KD = 6

C0 = (0, 64)
C1 = (64, 64)
C3 = (192, 64)
C2A = (128, 32)
C2B = (160, 32)


def gelu_pair(value, grad):
    square = value * value
    inner = TANH_SCALE * value * (1.0 + CUBIC * square)
    tangent = jnp.tanh(inner)
    half = 0.5 * (1.0 + tangent)
    act = value * half
    slope = half + 0.5 * value * (1.0 - tangent * tangent) * TANH_SCALE * (1.0 + 3.0 * CUBIC * square)
    return act, grad * slope


def dot_nn(a, b):
    return lax.dot_general(a, b, (((1,), (0,)), ((), ())), preferred_element_type=F32)


def dot_nt(a, b):
    return lax.dot_general(a, b, (((1,), (1,)), ((), ())), preferred_element_type=F32)


def al(value, unit=BLK):
    return pl.multiple_of(value, unit)


NAMES = (
    ["x%d" % d for d in range(8)]
    + ["g1a_m", "g1a_p", "g1b_m", "g1b_p", "g2_m", "g2_p"]
    + [k + str(c[0]) for k in ("sib", "xlo", "act", "rs") for c in (C0, C1, C3, C2A, C2B)]
    + ["f%d" % d for d in range(8)]
    + ["z"]
)
SEM = {name: i for i, name in enumerate(NAMES)}


def kernel(
    x_hbm, g_hbm, up_hbm, urow_hbm, ucnt_hbm, dn_hbm, drow_hbm, dcnt_hbm,
    recv_out, ug_out, dg_out,
    sx, sg, urow_v, ucnt_v, drow_v, dcnt_v, tab, tab_s,
    own, gat, xa, ga, xt, upr, dnr, uden, dden, hpo, ss, sr, qs, qr, ah, act_t, ugs, dgs,
    ip, rsr, xs, xr, zs, zr,
    lsem, ssem, rsem,
):
    sec = lax.axis_index("section")
    row = lax.axis_index("row")
    col = lax.axis_index("col")
    n_sec = lax.axis_size("section")
    core = lax.rem(row, 2)
    y = lax.rem(col, 4)
    xhi4 = col - y
    me = xhi4 + row

    def at_y(step):
        return {"section": sec, "row": row, "col": xhi4 + lax.rem(y + step, 4)}

    def mate(g):
        r = lax.rem(g, 4)
        return {"section": sec, "row": r, "col": (g - r) + y}

    y_p, y_m, y_2 = at_y(1), at_y(3), at_y(2)
    sibling = {"section": sec, "row": row + 1 - 2 * core, "col": col}
    across = {"section": sec, "row": lax.rem(row + 2, 4), "col": col}
    z_m = {"section": lax.rem(sec + n_sec - 1, n_sec), "row": row, "col": col}
    z_p = {"section": lax.rem(sec + 1, n_sec), "row": row, "col": col}
    mates = [lax.rem(me + d, 8) for d in range(8)]

    barrier = pltpu.get_barrier_semaphore()
    for d in range(1, 8):
        pl.semaphore_signal(barrier, inc=1, device_id=mate(mates[d]), device_id_type=MESH)
    for dev in (y_p, y_m, y_2, z_p):
        pl.semaphore_signal(barrier, inc=1, device_id=dev, device_id_type=MESH)

    loads = []
    for i, (src, dst) in enumerate(
        [
            (x_hbm, sx), (g_hbm, sg), (urow_hbm, urow_v), (ucnt_hbm, ucnt_v), (drow_hbm, drow_v), (dcnt_hbm, dcnt_v),
            (up_hbm.at[0, pl.ds(0, BLK), :], upr.at[0]), (up_hbm.at[0, pl.ds(BLK, BLK), :], upr.at[1]),
            (up_hbm.at[0, pl.ds(2 * BLK, BLK), :], upr.at[2]),
            *((dn_hbm.at[0, pl.ds(k * BLK, BLK), :], dnr.at[k]) for k in range(KD)),
        ]
    ):
        copy = pltpu.make_async_copy(src, dst, lsem.at[i])
        copy.start()
        loads.append(copy)

    upr[KU] = jnp.zeros((BLK, HW), BF16)
    dnr[KD] = jnp.zeros((BLK, TW), BF16)
    act_t[CB] = jnp.zeros((BLK, TOK), BF16)
    xt[RB] = jnp.zeros((BLK, TOK), BF16)
    tab[...] = jnp.zeros(tab.shape, jnp.int32)

    loads[0].wait()
    loads[1].wait()
    xv = sx[0].astype(F32)
    gv = sg[0].astype(F32)
    for r in range(4):
        cols = slice(r * TW, (r + 1) * TW)
        own[r] = jnp.concatenate([xv[:, cols], gv[:, cols]], axis=0).astype(BF16)

    for i in range(2, 6):
        loads[i].wait()
    urow, ucnt, drow, dcnt = urow_v[0], ucnt_v[0], drow_v[0], dcnt_v[0]
    io_u = lax.broadcasted_iota(jnp.int32, (RB, CB), 0)
    inv_u = jnp.full((RB, CB), KU, jnp.int32)
    for k in range(KU):
        live = ucnt[0:1, :] > k
        target = urow[k:k + 1, :]
        inv_u = jnp.where((io_u == target) & live, k, inv_u)
        tab[pl.ds(16 + k, 1), pl.ds(0, CB)] = jnp.where(live, target, RB)
    tab[pl.ds(0, RB), pl.ds(0, CB)] = inv_u
    io_d = lax.broadcasted_iota(jnp.int32, (CB, RB), 0)
    inv_d = jnp.full((CB, RB), KD, jnp.int32)
    for k in range(KD):
        live = dcnt[0:1, :] > k
        target = drow[k:k + 1, :]
        inv_d = jnp.where((io_d == target) & live, k, inv_d)
        tab[pl.ds(48 + k, 1), pl.ds(0, RB)] = jnp.where(live, target, CB)
    tab[pl.ds(24, CB), pl.ds(0, RB)] = inv_d
    tab_copy = pltpu.make_async_copy(tab, tab_s, lsem.at[15])
    tab_copy.start()

    sent = []

    def remote(name, src, dst, dev, recv=None):
        return pltpu.make_async_remote_copy(
            src_ref=src, dst_ref=dst, send_sem=ssem.at[SEM[name]],
            recv_sem=rsem.at[SEM[name] if recv is None else recv],
            device_id=dev, device_id_type=MESH,
        )

    def send(*args, **kw):
        copy = remote(*args, **kw)
        copy.start()
        sent.append(copy)

    pl.semaphore_wait(barrier, 11)

    for d in (1, 7, 2, 6, 3, 5, 4):
        g = mates[d]
        send("x%d" % d, own.at[lax.rem(g, 4)], gat.at[0, me], mate(g), recv=SEM["x0"] + me)
    gat[0, me] = own[row]

    tab_copy.wait()
    for i in range(6, 9):
        loads[i].wait()

    def dense_up(j, carry):
        cols = pl.ds(al(j * BLK), BLK)
        for i in range(RB):
            uden[pl.ds(i * BLK, BLK), cols] = upr[tab_s[i, j], :, cols]
        return carry

    lax.fori_loop(0, CB, dense_up, 0)
    for i in range(9, 15):
        loads[i].wait()

    def dense_down(h, carry):
        rows = pl.ds(al(h * BLK), BLK)
        for j in range(RB):
            cols = pl.ds(j * BLK, BLK)
            dden[rows, cols] = dnr[tab_s[24 + h, j], :, cols]
        return carry

    lax.fori_loop(0, CB, dense_down, 0)

    for d in (1, 7, 2, 6, 3, 5, 4):
        g = mates[d]
        remote("x%d" % d, own.at[0], gat.at[0, g], mate(g), recv=SEM["x0"] + g).wait_recv()

    lo, hi = pl.ds(0, 4), pl.ds(4, 4)
    send("g1a_m", gat.at[0, lo], gat.at[1, lo], y_m)
    send("g1a_p", gat.at[0, hi], gat.at[2, hi], y_p)
    send("g1b_m", gat.at[0, hi], gat.at[1, hi], y_m)
    send("g1b_p", gat.at[0, lo], gat.at[2, lo], y_p)

    def arrived(name, ref):
        remote(name, ref, ref, y_p).wait_recv()

    def unpack(block):
        for g in range(8):
            v = gat[block, g].astype(F32)
            if g % 2 == 0:
                prev = v
            else:
                t = block * 64 + (g - 1) * SHARE
                xa[pl.ds(t, 16), :] = jnp.concatenate([prev[:SHARE], v[:SHARE]], axis=0).astype(BF16)
                ga[pl.ds(t, 16), :] = jnp.concatenate([prev[SHARE:], v[SHARE:]], axis=0).astype(BF16)

    NT = 512

    def forward(chunk):
        t, m = chunk
        rows = pl.ds(t, m)
        other = (1 - core) * HH

        def theirs(n, carry):
            c = al(n * NT)
            ss[0, rows, pl.ds(c, NT)] = dot_nn(xa[rows, :], uden[:, pl.ds(al(other + c), NT)]).astype(BF16)
            ss[1, rows, pl.ds(c, NT)] = dot_nt(ga[rows, :], dden[pl.ds(al(other + c), NT), :]).astype(BF16)
            return carry

        lax.fori_loop(0, HH // NT, theirs, 0)
        send("sib%d" % t, ss.at[:, rows, :], sr.at[:, rows, :], sibling)

        def ours(n, carry):
            c = al(n * NT)
            hpo[0, rows, pl.ds(c, NT)] = dot_nn(xa[rows, :], uden[:, pl.ds(al(core * HH + c), NT)])
            hpo[1, rows, pl.ds(c, NT)] = dot_nt(ga[rows, :], dden[pl.ds(al(core * HH + c), NT), :])
            return carry

        lax.fori_loop(0, HH // NT, ours, 0)

    def combine(chunk):
        t, m = chunk
        rows = pl.ds(t, m)
        arrived("sib%d" % t, sr.at[:, rows, :])

        def body(n, carry):
            cols = pl.ds(al(n * 256), 256)
            for kind in range(2):
                total = hpo[kind, rows, cols] + sr[kind, rows, cols].astype(F32)
                hpo[kind, rows, cols] = total
                qs[kind, rows, cols] = total.astype(BF16)
            return carry

        lax.fori_loop(0, HH // 256, body, 0)
        send("xlo%d" % t, qs.at[:, rows, :], qr.at[:, rows, :], across)

    def activate(chunk):
        t, m = chunk
        rows = pl.ds(t, m)
        arrived("xlo%d" % t, qr.at[:, rows, :])

        def body(n, carry):
            cols = pl.ds(al(n * BLK), BLK)
            hidden = hpo[0, rows, cols] + qr[0, rows, cols].astype(F32)
            grad = hpo[1, rows, cols] + qr[1, rows, cols].astype(F32)
            act, slope = gelu_pair(hidden, grad)
            ah[core, 0, rows, cols] = act.astype(BF16)
            ah[core, 1, rows, cols] = slope.astype(BF16)
            return carry

        lax.fori_loop(0, HH // BLK, body, 0)
        send("act%d" % t, ah.at[core, :, rows, :], ah.at[core, :, rows, :], sibling)

    def backward(chunk):
        t, m = chunk
        rows = pl.ds(t, m)
        arrived("act%d" % t, ah.at[1 - core, :, rows, :])

        def body(n, carry):
            c = pl.ds(al(n * 256), 256)
            part = dot_nt(ah[0, 1, rows, :], uden[c, pl.ds(0, HH)]) + dot_nt(ah[1, 1, rows, :], uden[c, pl.ds(HH, HH)])
            ip[rows, c] = part.astype(BF16)
            return carry

        lax.fori_loop(0, TW // 256, body, 0)
        block = t // 64
        if block > 0:
            dev = (y_p, y_m, y_2)[block - 1]
            send("rs%d" % t, ip.at[rows, :], rsr.at[block - 1, pl.ds(t % 64, m), :], dev)

    unpack(0)
    forward(C0)
    combine(C0)
    arrived("g1a_m", gat.at[1, lo])
    send("g2_m", gat.at[1, lo], gat.at[3, lo], y_m)
    arrived("g1a_p", gat.at[2, hi])
    send("g2_p", gat.at[2, hi], gat.at[3, hi], y_p)
    arrived("g1b_m", gat.at[1, hi])
    unpack(1)
    forward(C1)
    combine(C1)
    activate(C0)
    backward(C0)
    arrived("g1b_p", gat.at[2, lo])
    unpack(2)
    arrived("g2_m", gat.at[3, lo])
    arrived("g2_p", gat.at[3, hi])
    unpack(3)
    forward(C3)
    combine(C3)
    activate(C1)
    backward(C1)
    forward(C2A)
    combine(C2A)
    forward(C2B)
    combine(C2B)

    def turn_x(i, carry):
        cols = pl.ds(al(i * BLK), BLK)
        xt[i] = xa[:, cols].T
        return carry

    lax.fori_loop(0, RB, turn_x, 0)
    activate(C3)
    backward(C3)
    activate(C2A)
    backward(C2A)
    activate(C2B)
    backward(C2B)

    for half in range(2):
        def turn_act(i, carry):
            act_t[half * RB + i] = ah[half, 0, :, pl.ds(al(i * BLK), BLK)].T
            return carry

        lax.fori_loop(0, RB, turn_act, 0)

    def down_grad(j, carry):
        cols = pl.ds(al(j * BLK), BLK)
        picked = [act_t[tab_s[48 + k, j]] for k in range(KD)]
        dgs[:, cols] = dot_nn(jnp.concatenate(picked, axis=0), ga[:, cols]).astype(BF16)
        return carry

    lax.fori_loop(0, RB, down_grad, 0)
    dg_copy = pltpu.make_async_copy(dgs, dg_out.at[0], lsem.at[0])
    dg_copy.start()

    for t, m in (C1, C2A, C2B, C3):
        arrived("rs%d" % t, rsr.at[t // 64 - 1, pl.ds(t % 64, m), :])
    for g in range(0, 8, 2):
        rows = pl.ds(g * SHARE, 2 * SHARE)
        total = ip[rows, :].astype(F32)
        for b in range(3):
            total = total + rsr[b, rows, :].astype(F32)
        for i in range(2):
            v = total[i * SHARE:(i + 1) * SHARE]
            xs[g + i] = jnp.concatenate([v[:, :TW // 2], v[:, TW // 2:]], axis=0).astype(BF16)
    for d in (4, 2, 6, 3, 5, 1, 7):
        g = mates[d]
        send("f%d" % d, xs.at[g], xr.at[me], mate(g), recv=SEM["f0"] + me)
    xr[me] = xs[me]

    for half in range(2):
        def up_grad(i, carry):
            j = half * RB + i
            weights = ah[half, 1, :, pl.ds(al(i * BLK), BLK)]
            picked = [xt[tab_s[16 + k, j]] for k in range(KU)]
            ugs[:, pl.ds(al(j * BLK), BLK)] = dot_nn(jnp.concatenate(picked, axis=0), weights).astype(BF16)
            return carry

        lax.fori_loop(0, RB, up_grad, 0)
    ug_copy = pltpu.make_async_copy(ugs, ug_out.at[0], lsem.at[1])
    ug_copy.start()

    for d in range(1, 8):
        g = mates[d]
        remote("f%d" % d, xs.at[0], xr.at[g], mate(g), recv=SEM["f0"] + g).wait_recv()
    for r in range(4):
        skip = sg[0, :, r * TW:(r + 1) * TW].astype(F32)
        skip = jnp.concatenate([skip[:, :TW // 2], skip[:, TW // 2:]], axis=0)
        zs[r] = (skip + (xr[r].astype(F32) + xr[4 + r].astype(F32))).astype(BF16)
    send("z", zs, zr, z_m)
    arrived("z", zr)
    keep = sec < n_sec - 1
    for r in range(4):
        v = jnp.where(keep, zr[r].astype(F32), 0.0)
        v = jnp.concatenate([v[:SHARE], v[SHARE:]], axis=1)
        recv_out[0, :, r * TW:(r + 1) * TW] = v.astype(BF16)
    dg_copy.wait()
    ug_copy.wait()
    for copy in sent:
        copy.wait_send()


def shards(layer_input, output_grad, up_panels, up_rows, up_counts, down_panels, down_rows, down_counts):
    hbm = pl.BlockSpec(memory_space=pl.ANY)
    vmem = pltpu.VMEM
    return pl.pallas_call(
        kernel,
        out_shape=(
            jax.ShapeDtypeStruct((1, SHARE, D), BF16),
            jax.ShapeDtypeStruct((1, KU * BLK, HW), BF16),
            jax.ShapeDtypeStruct((1, KD * BLK, TW), BF16),
        ),
        in_specs=[hbm] * 8,
        out_specs=(pl.BlockSpec(memory_space=pltpu.VMEM), hbm, hbm),
        scratch_shapes=[
            vmem((1, SHARE, D), BF16), vmem((1, SHARE, D), BF16),
            vmem((1, KU, CB), jnp.int32), vmem((1, 1, CB), jnp.int32),
            vmem((1, KD, RB), jnp.int32), vmem((1, 1, RB), jnp.int32),
            vmem((64, 128), jnp.int32), pltpu.SMEM((64, 128), jnp.int32),
            vmem((4, 2 * SHARE, TW), BF16),
            vmem((4, 8, 2 * SHARE, TW), BF16),
            vmem((TOK, TW), BF16), vmem((TOK, TW), BF16),
            vmem((RB + 1, BLK, TOK), BF16),
            vmem((KU + 1, BLK, HW), BF16), vmem((KD + 1, BLK, TW), BF16),
            vmem((TW, HW), BF16), vmem((HW, TW), BF16),
            vmem((2, TOK, HH), F32),
            vmem((2, TOK, HH), BF16), vmem((2, TOK, HH), BF16),
            vmem((2, TOK, HH), BF16), vmem((2, TOK, HH), BF16),
            vmem((2, 2, TOK, HH), BF16),
            vmem((CB + 1, BLK, TOK), BF16),
            vmem((KU * BLK, HW), BF16), vmem((KD * BLK, TW), BF16),
            vmem((TOK, TW), BF16), vmem((3, 64, TW), BF16),
            vmem((8, 2 * SHARE, TW // 2), BF16), vmem((8, 2 * SHARE, TW // 2), BF16),
            vmem((4, 2 * SHARE, TW // 2), BF16), vmem((4, 2 * SHARE, TW // 2), BF16),
            pltpu.SemaphoreType.DMA((16,)),
            pltpu.SemaphoreType.DMA((len(NAMES),)),
            pltpu.SemaphoreType.DMA((len(NAMES),)),
        ],
        compiler_params=pltpu.CompilerParams(
            collective_id=0, has_side_effects=True, vmem_limit_bytes=60 * 1024 * 1024
        ),
    )(layer_input, output_grad, up_panels, up_rows, up_counts, down_panels, down_rows, down_counts)


def solution(mesh):
    in_specs = (
        P("section", ("row", "col"), None),
        P("section", ("row", "col"), None),
        P("section", "row", "col"),
        P("section", "row", "col"),
        P("section", "row", "col"),
        P("section", "col", "row"),
        P("section", "col", "row"),
        P("section", "col", "row"),
    )
    out_specs = (
        P("section", ("row", "col"), None),
        P("section", "row", "col"),
        P("section", "col", "row"),
    )
    return jax.shard_map(shards, mesh=mesh, in_specs=in_specs, out_specs=out_specs, check_vma=False)
```

time: 539 us -> 97.5 us (0.18); the launches traced: 533 us -> 97.4 us
  waiting for transfers between devices: 374 us -> 0 us
  Pallas kernels: 0 us -> 87.9 us
  local copies, waits for them, and re-layouts: 76.2 us -> 8.86 us
  other arithmetic: 35.9 us -> 0 us
  matrix products: 30.7 us -> 0 us
  between operations: 14.4 us -> 0.64 us
    all_gather x4 -> x0, waiting for transfers between devices: 205 us -> none  [the longest x1 90.4 us: shards(): lax.all_gather(own_input, ('row', 'col'), axis=0, tiled=True)]
    reduce_scatter x3 -> x0, waiting for transfers between devices: 166 us -> none  [the longest x1 139 us: shards(): lax.psum_scatter(lax.dynamic_update_slice_in_dim(padded, placed.reshape(h...]
    pallas_call x0 -> x1, Pallas kernels: none -> 87.9 us  [shards(): pl.pallas_call(kernel, out_shape=(jax.ShapeDtypeStruct((1, SHARE, D), BF1...]
    dot_general x5 -> x0, matrix products: 30.7 us -> none  [the longest x1 7.72 us: shards(): jnp.einsum('tjq,kpjq->tkjp', picked, down_masked, preferred_element_type=...]
    scatter-add x2 -> x0, other arithmetic: 30.1 us -> none  [the longest x1 15.1 us: shards(): placed = jnp.zeros((hidden_blocks.shape[0], row_blocks, BLK), jnp.float32...]
    transpose x2 -> x0, local copies, waits for them, and re-layouts: 19.3 us -> none  [the longest x1 9.65 us: shards(): jnp.einsum('tjq,kpjq->tkjp', picked, down_masked, preferred_element_type=...]
    another operation x5 -> x0, local copies, waits for them, and re-layouts: 15.6 us -> none  [the longest x2 7.45 us: shards(): down_view = down_panels[0].reshape(down_slots, BLK, row_blocks, BLK)]
    gather x2 -> x0, local copies, waits for them, and re-layouts: 11 us -> none  [the longest x1 5.54 us: shards(): jnp.take(input_rows.reshape(all_tokens, row_blocks, BLK), up_targets, axi...]
  transfers between devices with their start and end apart: 8 -> 0, of which waited for: 5 -> 0; matrix products, arithmetic and copies ran while one was open for 22% -> 0% of each run, Pallas kernels for 0% -> 0%
where the time goes in v1:
time: 97.5 us; the launch traced here: 97.4 us
  Pallas kernels  87.9 us (90%)
  local copies, waits for them, and re-layouts  8.86 us (9%)
    pallas_call x1, Pallas kernels, shards(): pl.pallas_call(kernel, out_shape=(jax.ShapeDtypeStruct((1, SHARE, D), BF1...  87.9 us
    unnamed x7, local copies, waits for them, and re-layouts  8.86 us

profile of v1, /device:TPU:1, one launch (start us, length us, event | category | flops | bytes accessed | tf_op | source)
XLA Modules:
  0.0 97.4 jit_solution(11155471949905114690)
XLA Ops:
  0.6 1.3 %copy.11.urow_hbm = s32[1,3,24]{2,1,0:T(4,128)} copy(s32[1,3,24]{2,0,1:T(1,128)} %param.11) | data formatting | bytes 576 | tf_op args[3]
  1.9 1.3 %copy.12.drow_hbm = s32[1,6,12]{2,1,0:T(8,128)} copy(s32[1,6,12]{2,0,1:T(1,128)} %param.14) | data formatting | bytes 576 | tf_op args[6]
  3.2 87.9 %shard_map.103 = (bf16[1,8,6144]{2,1,0:T(8,128)(2,1)}, bf16[1,384,3072]{2,1,0:T(8,128)(2,1)}, bf16[1,768,1536]{2,1,0:T(8,128)(2,1)}) custom-call(bf16[1,8,6144]{2,1,0:T(8,128)(2,1)} %x_hbm.1, bf16[1,8,6144]{2,1,0:T(8,128)(2,1)} %g_hbm.1, bf16[1,384,3072]{2,1,0:T(8,128)(2,1)} %up_hbm.1, s32[1,3,24]{2,1,0:T(4,128)} %copy.11.urow_hbm, s32[1,1,24]{2,1,0:T(1,128)} %ucnt_hbm.1, ...), custom_call_target="tpu_custom_call" | custom-call | tf_op jit(solution)/shard_map/pallas_call | solution.py:402
  91.0 1.5 %copy.16 = bf16[1,8,6144]{2,1,0:T(8,128)(2,1)} copy(bf16[1,8,6144]{2,1,0:T(8,128)(2,1)} %get-tuple-element.6) | data formatting | bytes 196608
  92.6 0.0 copy-start
  92.6 3.4 %copy.17 = bf16[1,384,3072]{2,1,0:T(8,128)(2,1)} copy(bf16[1,384,3072]{2,1,0:T(8,128)(2,1)} %get-tuple-element.7) | data formatting | bytes 4718592
  96.0 0.0 copy-done
  96.0 1.4 %copy.18 = bf16[1,768,1536]{2,1,0:T(8,128)(2,1)} copy(bf16[1,768,1536]{2,1,0:T(8,128)(2,1)S(1)} %copy-done) | data formatting | bytes 4718592
Async XLA Ops:
  92.6 3.4 %copy-start = (bf16[1,768,1536]{2,1,0:T(8,128)(2,1)S(1)}, bf16[1,768,1536]{2,1,0:T(8,128)(2,1)}, u32[]{:S(2)}) copy-start(bf16[1,768,1536]{2,1,0:T(8,128)(2,1)} %get-tuple-element.8) | copy-start | bytes 7077892

commit v2 on v1

v2 whole, which is shorter than its diff:
```python
import functools
import math

import jax
import jax.numpy as jnp
from jax import lax
from jax.experimental import pallas as pl
from jax.experimental.pallas import tpu as pltpu
from jax.sharding import PartitionSpec as P

BLK = 128
TANH_SCALE = math.sqrt(2.0 / math.pi)
CUBIC = 0.044715
MESH = pl.DeviceIdType.MESH
F32 = jnp.float32
BF16 = jnp.bfloat16

TOK = 256
SHARE = 8
TW = 1536
HW = 3072
HH = HW // 2
D = 4 * TW
RB = TW // BLK
CB = HW // BLK
KU = 3
KD = 6

CA = (0, 64)
CB1 = (64, 64)
CD = (128, 64)
CC = (192, 64)
CE = (128, 128)
START = {(0, 0): 0, (0, 1): 32, (1, 0): 64, (2, 0): 96, (1, 1): 128, (2, 1): 160, (3, 0): 192, (3, 1): 224}


def gelu_pair(value, grad):
    square = value * value
    inner = TANH_SCALE * value * (1.0 + CUBIC * square)
    tangent = jnp.tanh(inner)
    half = 0.5 * (1.0 + tangent)
    act = value * half
    slope = half + 0.5 * value * (1.0 - tangent * tangent) * TANH_SCALE * (1.0 + 3.0 * CUBIC * square)
    return act, grad * slope


def dot_nn(a, b):
    return lax.dot_general(a, b, (((1,), (0,)), ((), ())), preferred_element_type=F32)


def dot_nt(a, b):
    return lax.dot_general(a, b, (((1,), (1,)), ((), ())), preferred_element_type=F32)


def al(value, unit=BLK):
    return pl.multiple_of(value, unit)


NAMES = (
    ["x%d" % d for d in range(8)]
    + ["g1a_m", "g1a_p", "g1b_m", "g1b_p", "g2_m", "g2_p", "zg"]
    + ["sib%d_%d" % (c[0], k) for c in (CA, CB1, CE) for k in range(2)]
    + ["xlo%d_%d" % (c[0], k) for c in (CA, CB1, CC, CD) for k in range(2)]
    + ["act%d" % c[0] for c in (CA, CB1, CC, CD)]
    + ["rs%d_%d_%d" % (b, h, n) for b in range(4) for h in range(2) for n in range(2)]
    + ["f%d" % d for d in range(8)]
)
SEM = {name: i for i, name in enumerate(NAMES)}


def kernel(
    x_hbm, g_hbm, up_hbm, urow_hbm, ucnt_hbm, dn_hbm, drow_hbm, dcnt_hbm,
    recv_out, ug_out, dg_out,
    sx, sg, urow_v, ucnt_v, drow_v, dcnt_v, tab, tab_s,
    own, zown, gat, xa, ga, xt, upr, dnr, uden, dden, hpo, ss, sr, qs, qr, ah, act_t,
    ip, rsr, xs, xr,
    lsem, ssem, rsem,
):
    sec = lax.axis_index("section")
    row = lax.axis_index("row")
    col = lax.axis_index("col")
    n_sec = lax.axis_size("section")
    core = lax.rem(row, 2)
    x_lo = row // 2
    y = lax.rem(col, 4)
    xhi4 = col - y
    me = core * 4 + xhi4 // 2 + x_lo
    before = lax.rem(sec + n_sec - 1, n_sec)
    after = lax.rem(sec + 1, n_sec)

    def at_y(step, section):
        return {"section": section, "row": row, "col": xhi4 + lax.rem(y + step, 4)}

    def mate(g):
        x = lax.rem(g, 4)
        return {"section": sec, "row": lax.rem(x, 2) * 2 + g // 4, "col": (x // 2) * 4 + y}

    def mate_row(g):
        return lax.rem(g, 2) * 2 + g // 4

    y_p, y_m = at_y(1, sec), at_y(3, sec)
    owners = [at_y(step, before) for step in (0, 1, 3, 2)]
    sibling = {"section": sec, "row": row + 1 - 2 * core, "col": col}
    across = {"section": sec, "row": lax.rem(row + 2, 4), "col": col}
    mates = [lax.rem(me + d, 8) for d in range(8)]

    barrier = pltpu.get_barrier_semaphore()
    for d in range(1, 8):
        pl.semaphore_signal(barrier, inc=1, device_id=mate(mates[d]), device_id_type=MESH)
    for dev in [y_p, y_m] + [at_y(step, after) for step in range(4)]:
        pl.semaphore_signal(barrier, inc=1, device_id=dev, device_id_type=MESH)

    loads = []
    for i, (src, dst) in enumerate(
        [
            (x_hbm, sx), (g_hbm, sg), (urow_hbm, urow_v), (ucnt_hbm, ucnt_v), (drow_hbm, drow_v), (dcnt_hbm, dcnt_v),
            *((up_hbm.at[0, pl.ds(k * BLK, BLK), :], upr.at[k]) for k in range(KU)),
            *((dn_hbm.at[0, pl.ds(k * BLK, BLK), :], dnr.at[k]) for k in range(KD)),
        ]
    ):
        copy = pltpu.make_async_copy(src, dst, lsem.at[i])
        copy.start()
        loads.append(copy)

    loads[0].wait()
    loads[1].wait()
    xv = sx[0].astype(F32)
    gv = sg[0].astype(F32)
    for r in range(4):
        cols = slice(r * TW, (r + 1) * TW)
        own[r] = jnp.concatenate([xv[:, cols], gv[:, cols]], axis=0).astype(BF16)

    sent = []

    def remote(name, src, dst, dev, recv=None):
        return pltpu.make_async_remote_copy(
            src_ref=src, dst_ref=dst, send_sem=ssem.at[SEM[name]],
            recv_sem=rsem.at[SEM[name] if recv is None else recv],
            device_id=dev, device_id_type=MESH,
        )

    def send(*args, **kw):
        copy = remote(*args, **kw)
        copy.start()
        sent.append(copy)

    def arrived(name, ref):
        remote(name, ref, ref, y_p).wait_recv()

    pl.semaphore_wait(barrier, 13)

    for d in (1, 7, 2, 6, 3, 5, 4):
        g = mates[d]
        send("x%d" % d, own.at[mate_row(g)], gat.at[0, me], mate(g), recv=SEM["x0"] + me)
    send("zg", own, zown, owners[0])
    gat[0, me] = own[row]

    upr[KU] = jnp.zeros((BLK, HW), BF16)
    dnr[KD] = jnp.zeros((BLK, TW), BF16)
    act_t[CB] = jnp.zeros((BLK, TOK), BF16)
    xt[RB] = jnp.zeros((BLK, TOK), BF16)
    tab[...] = jnp.zeros(tab.shape, jnp.int32)
    for i in range(2, 6):
        loads[i].wait()
    ucnt, dcnt = ucnt_v[0], dcnt_v[0]
    io_u = lax.broadcasted_iota(jnp.int32, (RB, CB), 0)
    inv_u = jnp.full((RB, CB), KU, jnp.int32)
    for k in range(KU):
        live = ucnt > k
        target = urow_v[k]
        inv_u = jnp.where((io_u == target) & live, k, inv_u)
        tab[pl.ds(16 + k, 1), pl.ds(0, CB)] = jnp.where(live, target, RB)
    tab[pl.ds(0, RB), pl.ds(0, CB)] = inv_u
    io_d = lax.broadcasted_iota(jnp.int32, (CB, RB), 0)
    inv_d = jnp.full((CB, RB), KD, jnp.int32)
    for k in range(KD):
        live = dcnt > k
        target = drow_v[k]
        inv_d = jnp.where((io_d == target) & live, k, inv_d)
        tab[pl.ds(48 + k, 1), pl.ds(0, RB)] = jnp.where(live, target, CB)
    tab[pl.ds(24, CB), pl.ds(0, RB)] = inv_d
    tab_copy = pltpu.make_async_copy(tab, tab_s, lsem.at[15])
    tab_copy.start()

    for i in range(6, 9):
        loads[i].wait()
    tab_copy.wait()

    def dense_up(j, carry):
        cols = pl.ds(al(j * BLK), BLK)
        for i in range(RB):
            uden[pl.ds(i * BLK, BLK), cols] = upr[tab_s[i, j], :, cols]
        return carry

    lax.fori_loop(0, CB, dense_up, 0)
    for i in range(9, 15):
        loads[i].wait()

    def dense_down(h, carry):
        rows = pl.ds(al(h * BLK), BLK)
        for j in range(RB):
            cols = pl.ds(j * BLK, BLK)
            dden[rows, cols] = dnr[tab_s[24 + h, j], :, cols]
        return carry

    lax.fori_loop(0, CB, dense_down, 0)

    for d in (1, 7, 2, 6, 3, 5, 4):
        g = mates[d]
        remote("x%d" % d, own.at[0], gat.at[0, g], mate(g), recv=SEM["x0"] + g).wait_recv()

    lo, hi = pl.ds(0, 4), pl.ds(4, 4)
    send("g1a_m", gat.at[0, lo], gat.at[1, lo], y_m)
    send("g1a_p", gat.at[0, lo], gat.at[2, lo], y_p)
    send("g1b_p", gat.at[0, hi], gat.at[2, hi], y_p)
    send("g1b_m", gat.at[0, hi], gat.at[1, hi], y_m)

    def unpack(block, half):
        for i in range(2):
            a = gat[block, half * 4 + 2 * i].astype(F32)
            b = gat[block, half * 4 + 2 * i + 1].astype(F32)
            rows = pl.ds(START[block, half] + 16 * i, 16)
            xa[rows, :] = jnp.concatenate([a[:SHARE], b[:SHARE]], axis=0).astype(BF16)
            ga[rows, :] = jnp.concatenate([a[SHARE:], b[SHARE:]], axis=0).astype(BF16)

    NT = 512

    def product(kind, rows, c):
        if kind == 0:
            return dot_nn(xa[rows, :], uden[:, pl.ds(c, NT)])
        return dot_nt(ga[rows, :], dden[pl.ds(c, NT), :])

    def forward(chunk, kind):
        t, m = chunk
        rows = pl.ds(t, m)
        other = (1 - core) * HH

        def theirs(n, carry):
            ss[kind, rows, pl.ds(al(n * NT), NT)] = product(kind, rows, al(other + n * NT)).astype(BF16)
            return carry

        lax.fori_loop(0, HH // NT, theirs, 0)
        send("sib%d_%d" % (t, kind), ss.at[kind, rows, :], sr.at[kind, rows, :], sibling)

        def ours(n, carry):
            hpo[kind, rows, pl.ds(al(n * NT), NT)] = product(kind, rows, al(core * HH + n * NT))
            return carry

        lax.fori_loop(0, HH // NT, ours, 0)
        arrived("sib%d_%d" % (t, kind), sr.at[kind, rows, :])

    def combine(chunk, kind):
        t, m = chunk
        rows = pl.ds(t, m)

        def body(n, carry):
            cols = pl.ds(al(n * 256), 256)
            total = hpo[kind, rows, cols] + sr[kind, rows, cols].astype(F32)
            hpo[kind, rows, cols] = total
            qs[kind, rows, cols] = total.astype(BF16)
            return carry

        lax.fori_loop(0, HH // 256, body, 0)
        send("xlo%d_%d" % (t, kind), qs.at[kind, rows, :], qr.at[kind, rows, :], across)

    def activate(chunk):
        t, m = chunk
        rows = pl.ds(t, m)
        for kind in range(2):
            arrived("xlo%d_%d" % (t, kind), qr.at[kind, rows, :])

        def body(n, carry):
            cols = pl.ds(al(n * BLK), BLK)
            hidden = hpo[0, rows, cols] + qr[0, rows, cols].astype(F32)
            grad = hpo[1, rows, cols] + qr[1, rows, cols].astype(F32)
            act, slope = gelu_pair(hidden, grad)
            ah[core, 0, rows, cols] = act.astype(BF16)
            ah[core, 1, rows, cols] = slope.astype(BF16)
            return carry

        lax.fori_loop(0, HH // BLK, body, 0)
        send("act%d" % t, ah.at[core, :, rows, :], ah.at[core, :, rows, :], sibling)

    def backward(chunk, parts):
        t, m = chunk
        rows = pl.ds(t, m)
        arrived("act%d" % t, ah.at[1 - core, :, rows, :])
        for n in range(2):
            c = pl.ds(n * (TW // 2), TW // 2)
            part = dot_nt(ah[0, 1, rows, :], uden[c, pl.ds(0, HH)]) + dot_nt(ah[1, 1, rows, :], uden[c, pl.ds(HH, HH)])
            ip[n, rows, :] = part.astype(BF16)
            for b, h in parts:
                send(
                    "rs%d_%d_%d" % (b, h, n), ip.at[n, pl.ds(START[b, h], 32), :],
                    rsr.at[b, n, pl.ds(32 * h, 32), :], owners[b],
                )

    unpack(0, 0)
    unpack(0, 1)
    forward(CA, 0)
    combine(CA, 0)
    forward(CA, 1)
    combine(CA, 1)
    arrived("g1a_m", gat.at[1, lo])
    send("g2_m", gat.at[1, lo], gat.at[3, lo], y_m)
    arrived("g1a_p", gat.at[2, lo])
    unpack(1, 0)
    unpack(2, 0)
    forward(CB1, 0)
    combine(CB1, 0)
    arrived("g1b_p", gat.at[2, hi])
    send("g2_p", gat.at[2, hi], gat.at[3, hi], y_p)
    forward(CB1, 1)
    combine(CB1, 1)
    arrived("g1b_m", gat.at[1, hi])
    unpack(1, 1)
    unpack(2, 1)
    activate(CA)
    backward(CA, ((0, 0), (0, 1)))
    arrived("g2_m", gat.at[3, lo])
    arrived("g2_p", gat.at[3, hi])
    unpack(3, 0)
    unpack(3, 1)
    forward(CE, 0)
    combine(CC, 0)
    forward(CE, 1)
    combine(CC, 1)
    combine(CD, 0)
    combine(CD, 1)
    activate(CB1)
    backward(CB1, ((1, 0), (2, 0)))

    def turn_x(i, carry):
        xt[i] = xa[:, pl.ds(al(i * BLK), BLK)].T
        return carry

    lax.fori_loop(0, RB, turn_x, 0)

    def turn_acts(first):
        for half in range(2):
            def turn_act(i, carry):
                block = ah[half, 0, pl.ds(first, 128), pl.ds(al(i * BLK), BLK)]
                act_t[half * RB + i, :, pl.ds(first, 128)] = block.T
                return carry

            lax.fori_loop(0, RB, turn_act, 0)

    turn_acts(0)
    activate(CC)
    backward(CC, ((3, 0), (3, 1)))

    order = [lax.rem(me + d, 4) for d in range(4)]

    def finish(h):
        for b in range(4):
            for n in range(2):
                arrived("rs%d_%d_%d" % (b, h, n), rsr.at[b, n, pl.ds(32 * h, 32), :])
        for i in range(2):
            rows = pl.ds(32 * h + 16 * i, 16)
            for n in range(2):
                total = rsr[0, n, rows, :].astype(F32)
                for b in range(1, 4):
                    total = total + rsr[b, n, rows, :].astype(F32)
                halves.append(total)
            left, right = halves[-2], halves[-1]
            for k in range(2):
                span = slice(k * SHARE, (k + 1) * SHARE)
                xs[4 * h + 2 * i + k] = jnp.concatenate([left[span], right[span]], axis=0).astype(BF16)
        for k in range(4):
            g = order[k] + 4 * h

            @pl.when(g != me)
            def _():
                remote("f%d" % (4 * h + k), xs.at[g], xr.at[me], mate(g), recv=SEM["f0"] + me).start()

            @pl.when(g == me)
            def _():
                xr[me] = xs[me]

    halves = []

    def down_grad(j, carry):
        cols = pl.ds(al(j * BLK), BLK)
        picked = [act_t[tab_s[48 + k, j]] for k in range(KD)]
        dg_out[0, :, cols] = dot_nn(jnp.concatenate(picked, axis=0), ga[:, cols]).astype(BF16)
        return carry

    def up_grads(half):
        def up_grad(i, carry):
            j = half * RB + i
            weights = ah[half, 1, :, pl.ds(al(i * BLK), BLK)]
            picked = [xt[tab_s[16 + k, j]] for k in range(KU)]
            ug_out[0, :, pl.ds(al(j * BLK), BLK)] = dot_nn(jnp.concatenate(picked, axis=0), weights).astype(BF16)
            return carry

        lax.fori_loop(0, RB, up_grad, 0)

    activate(CD)
    finish(0)
    backward(CD, ((1, 1), (2, 1)))
    up_grads(0)
    finish(1)
    up_grads(1)
    turn_acts(128)
    lax.fori_loop(0, RB, down_grad, 0)

    for d in range(1, 8):
        g = mates[d]
        remote("f%d" % d, xs.at[0], xr.at[g], mate(g), recv=SEM["f0"] + g).wait_recv()
    arrived("zg", zown)
    keep = sec < n_sec - 1
    for r in range(4):
        base = zown[r].astype(F32)[SHARE:]
        base = jnp.concatenate([base[:, :TW // 2], base[:, TW // 2:]], axis=0)
        first = (r % 2) * 4 + r // 2
        v = (base + (xr[first].astype(F32) + xr[first + 2].astype(F32)))
        v = jnp.where(keep, v, 0.0)
        recv_out[0, :, r * TW:(r + 1) * TW] = jnp.concatenate([v[:SHARE], v[SHARE:]], axis=1).astype(BF16)
    for copy in sent:
        copy.wait_send()
    for h in range(2):
        for k in range(4):
            g = order[k] + 4 * h

            @pl.when(g != me)
            def _():
                remote("f%d" % (4 * h + k), xs.at[g], xr.at[me], mate(g), recv=SEM["f0"] + me).wait_send()


def shards(layer_input, output_grad, up_panels, up_rows, up_counts, down_panels, down_rows, down_counts):
    hbm = pl.BlockSpec(memory_space=pl.ANY)
    vmem = pltpu.VMEM
    return pl.pallas_call(
        kernel,
        out_shape=(
            vmem((1, SHARE, D), BF16), vmem((1, KU * BLK, HW), BF16), vmem((1, KD * BLK, TW), BF16),
        ),
        in_specs=[hbm] * 8,
        out_specs=(pl.BlockSpec(memory_space=pltpu.VMEM),) * 3,
        scratch_shapes=[
            vmem((1, SHARE, D), BF16), vmem((1, SHARE, D), BF16),
            vmem((KU, 1, CB), jnp.int32), vmem((1, 1, CB), jnp.int32),
            vmem((KD, 1, RB), jnp.int32), vmem((1, 1, RB), jnp.int32),
            vmem((64, 128), jnp.int32), pltpu.SMEM((64, 128), jnp.int32),
            vmem((4, 2 * SHARE, TW), BF16), vmem((4, 2 * SHARE, TW), BF16),
            vmem((4, 8, 2 * SHARE, TW), BF16),
            vmem((TOK, TW), BF16), vmem((TOK, TW), BF16),
            vmem((RB + 1, BLK, TOK), BF16),
            vmem((KU + 1, BLK, HW), BF16), vmem((KD + 1, BLK, TW), BF16),
            vmem((TW, HW), BF16), vmem((HW, TW), BF16),
            vmem((2, TOK, HH), F32),
            vmem((2, TOK, HH), BF16), vmem((2, TOK, HH), BF16),
            vmem((2, TOK, HH), BF16), vmem((2, TOK, HH), BF16),
            vmem((2, 2, TOK, HH), BF16),
            vmem((CB + 1, BLK, TOK), BF16),
            vmem((2, TOK, TW // 2), BF16), vmem((4, 2, 64, TW // 2), BF16),
            vmem((8, 2 * SHARE, TW // 2), BF16), vmem((8, 2 * SHARE, TW // 2), BF16),
            pltpu.SemaphoreType.DMA((16,)),
            pltpu.SemaphoreType.DMA((len(NAMES),)),
            pltpu.SemaphoreType.DMA((len(NAMES),)),
        ],
        compiler_params=pltpu.CompilerParams(
            collective_id=0, has_side_effects=True, vmem_limit_bytes=50 * 1024 * 1024
        ),
    )(
        layer_input, output_grad, up_panels, jnp.swapaxes(up_rows, 0, 1), up_counts,
        down_panels, jnp.swapaxes(down_rows, 0, 1), down_counts,
    )


def solution(mesh):
    in_specs = (
        P("section", ("row", "col"), None),
        P("section", ("row", "col"), None),
        P("section", "row", "col"),
        P("section", "row", "col"),
        P("section", "row", "col"),
        P("section", "col", "row"),
        P("section", "col", "row"),
        P("section", "col", "row"),
    )
    out_specs = (
        P("section", ("row", "col"), None),
        P("section", "row", "col"),
        P("section", "col", "row"),
    )
    return jax.shard_map(shards, mesh=mesh, in_specs=in_specs, out_specs=out_specs, check_vma=False)
```

time: 97.5 us -> 79.9 us (0.82)
  Pallas kernels: 87.9 us -> 75.1 us
  local copies, waits for them, and re-layouts: 8.86 us -> 3.45 us
    pallas_call x1, Pallas kernels: 87.9 us -> 75.1 us  [shards(): pl.pallas_call(kernel, out_shape=(vmem((1, SHARE, D), BF16), vmem((1, KU...]
    unnamed x7 -> x3, local copies, waits for them, and re-layouts: 8.86 us -> 3.45 us
where the time goes in v2:
time: 79.9 us; the launch traced here: 79.2 us
  Pallas kernels  75.1 us (94%)
  local copies, waits for them, and re-layouts  3.45 us (4%)
    pallas_call x1, Pallas kernels, shards(): pl.pallas_call(kernel, out_shape=(vmem((1, SHARE, D), BF16), vmem((1, KU...  75.1 us
    unnamed x3, local copies, waits for them, and re-layouts  3.45 us

profile of v2, /device:TPU:1, one launch (start us, length us, event | category | flops | bytes accessed | tf_op | source)
XLA Modules:
  0.0 79.2 jit_solution(1278367367360796655)
XLA Ops:
  0.6 75.1 %shard_map.103 = (bf16[1,8,6144]{2,1,0:T(8,128)(2,1)S(1)}, bf16[1,384,3072]{2,1,0:T(8,128)(2,1)S(1)}, bf16[1,768,1536]{2,1,0:T(8,128)(2,1)S(1)}) custom-call(bf16[1,8,6144]{2,1,0:T(8,128)(2,1)} %x_hbm.1, bf16[1,8,6144]{2,1,0:T(8,128)(2,1)} %g_hbm.1, bf16[1,384,3072]{2,1,0:T(8,128)(2,1)} %up_hbm.1, s32[3,1,24]{2,1,0:T(1,128)} %bitcast.3, ...), custom_call_target="tpu_custom_call" | custom-call | tf_op jit(solution)/shard_map/pallas_call | solution.py:433
  75.7 0.6 copy.14
  76.3 1.4 %copy.15 = bf16[1,384,3072]{2,1,0:T(8,128)(2,1)} copy(bf16[1,384,3072]{2,1,0:T(8,128)(2,1)S(1)} %get-tuple-element.4) | data formatting | bytes 4718592
  77.8 1.4 %copy.16 = bf16[1,768,1536]{2,1,0:T(8,128)(2,1)} copy(bf16[1,768,1536]{2,1,0:T(8,128)(2,1)S(1)} %get-tuple-element.5) | data formatting | bytes 4718592

commit v3 on v2

v3 whole, which is shorter than its diff:
```python
import functools
import math

import jax
import jax.numpy as jnp
from jax import lax
from jax.experimental import pallas as pl
from jax.experimental.pallas import tpu as pltpu
from jax.sharding import PartitionSpec as P

BLK = 128
TANH_SCALE = math.sqrt(2.0 / math.pi)
CUBIC = 0.044715
MESH = pl.DeviceIdType.MESH
F32 = jnp.float32
BF16 = jnp.bfloat16

TOK = 256
SHARE = 8
TW = 1536
HW = 3072
HH = HW // 2
D = 4 * TW
QW = HH // 2
RB = TW // BLK
CB = HW // BLK
KU = 3
KD = 6

CA = (0, 64)
CB1 = (64, 64)
CD = (128, 64)
CC = (192, 64)
CE = (128, 128)
START = {(0, 0): 0, (0, 1): 32, (1, 0): 64, (2, 0): 96, (1, 1): 128, (2, 1): 160, (3, 0): 192, (3, 1): 224}


def gelu_pair(value, grad):
    square = value * value
    inner = TANH_SCALE * value * (1.0 + CUBIC * square)
    tangent = jnp.tanh(inner)
    half = 0.5 * (1.0 + tangent)
    act = value * half
    slope = half + 0.5 * value * (1.0 - tangent * tangent) * TANH_SCALE * (1.0 + 3.0 * CUBIC * square)
    return act, grad * slope


def dot_nn(a, b):
    return lax.dot_general(a, b, (((1,), (0,)), ((), ())), preferred_element_type=F32)


def al(value, unit=BLK):
    return pl.multiple_of(value, unit)


NAMES = (
    ["x%d" % d for d in range(8)]
    + ["g1a_m", "g1a_p", "g1b_m", "g1b_p", "g2_m", "g2_p", "zg"]
    + ["sib%d_%d_%d" % (c[0], k, n) for c in (CA, CB1, CE) for k in range(2) for n in range(2)]
    + ["xlo%d_%d_%d" % (c[0], k, n) for c in (CA, CB1, CC, CD) for k in range(2) for n in range(2)]
    + ["act%d_%d" % (c[0], n) for c in (CA, CB1, CC, CD) for n in range(2)]
    + ["rs%d_%d_%d" % (b, h, n) for b in range(4) for h in range(2) for n in range(2)]
    + ["f%d" % d for d in range(8)]
)
SEM = {name: i for i, name in enumerate(NAMES)}


def kernel(
    x_hbm, g_hbm, up_hbm, urow_hbm, ucnt_hbm, dn_hbm, drow_hbm, dcnt_hbm,
    recv_out, ug_out, dg_out,
    sx, sg, urow_v, ucnt_v, drow_v, dcnt_v, tab, tab_s,
    own, zown, gat, xa, ga, xt, upr, dnr, upt, hpo, ss, sr, qs, qr, ah, act_t,
    ip, acc, rsr, xs, xr,
    lsem, ssem, rsem,
):
    sec = lax.axis_index("section")
    row = lax.axis_index("row")
    col = lax.axis_index("col")
    n_sec = lax.axis_size("section")
    core = lax.rem(row, 2)
    x_lo = row // 2
    y = lax.rem(col, 4)
    xhi4 = col - y
    me = core * 4 + xhi4 // 2 + x_lo
    before = lax.rem(sec + n_sec - 1, n_sec)
    after = lax.rem(sec + 1, n_sec)

    def at_y(step):
        return {"section": sec, "row": row, "col": xhi4 + lax.rem(y + step, 4)}

    def mate(g, section):
        x = lax.rem(g, 4)
        return {"section": section, "row": lax.rem(x, 2) * 2 + g // 4, "col": (x // 2) * 4 + y}

    def mate_row(g):
        return lax.rem(g, 2) * 2 + g // 4

    y_p, y_m, y_2 = at_y(1), at_y(3), at_y(2)
    sibling = {"section": sec, "row": row + 1 - 2 * core, "col": col}
    across = {"section": sec, "row": lax.rem(row + 2, 4), "col": col}
    mates = [lax.rem(me + d, 8) for d in range(8)]

    barrier = pltpu.get_barrier_semaphore()
    for d in range(1, 8):
        pl.semaphore_signal(barrier, inc=1, device_id=mate(mates[d], sec), device_id_type=MESH)
    for dev in [y_p, y_m, y_2] + [mate(mates[d], after) for d in range(8)]:
        pl.semaphore_signal(barrier, inc=1, device_id=dev, device_id_type=MESH)

    loads = []
    for i, (src, dst) in enumerate(
        [
            (x_hbm, sx), (g_hbm, sg), (urow_hbm, urow_v), (ucnt_hbm, ucnt_v), (drow_hbm, drow_v), (dcnt_hbm, dcnt_v),
            *((up_hbm.at[0, pl.ds(k * BLK, BLK), :], upr.at[k]) for k in range(KU)),
            *((dn_hbm.at[0, pl.ds(k * BLK, BLK), :], dnr.at[k]) for k in range(KD)),
        ]
    ):
        copy = pltpu.make_async_copy(src, dst, lsem.at[i])
        copy.start()
        loads.append(copy)

    loads[0].wait()
    loads[1].wait()
    xv = sx[0].astype(F32)
    gv = sg[0].astype(F32)
    for r in range(4):
        cols = slice(r * TW, (r + 1) * TW)
        own[r] = jnp.concatenate([xv[:, cols], gv[:, cols]], axis=0).astype(BF16)

    sent = []

    def remote(name, src, dst, dev, recv=None):
        return pltpu.make_async_remote_copy(
            src_ref=src, dst_ref=dst, send_sem=ssem.at[SEM[name]],
            recv_sem=rsem.at[SEM[name] if recv is None else recv],
            device_id=dev, device_id_type=MESH,
        )

    def send(*args, **kw):
        copy = remote(*args, **kw)
        copy.start()
        sent.append(copy)

    def arrived(name, ref):
        remote(name, ref, ref, y_p).wait_recv()

    def arrived_f(g):
        remote("f%d" % g, xs.at[g], xr.at[g], y_p).wait_recv()

    pl.semaphore_wait(barrier, 18)

    for d in (1, 7, 2, 6, 3, 5, 4):
        g = mates[d]
        send("x%d" % d, own.at[mate_row(g)], gat.at[0, me], mate(g, sec), recv=SEM["x0"] + me)
    send("zg", own, zown, mate(me, before))
    gat[0, me] = own[row]

    upr[KU] = jnp.zeros((BLK, HW), BF16)
    dnr[KD] = jnp.zeros((BLK, TW), BF16)
    act_t[CB] = jnp.zeros((BLK, TOK), BF16)
    xt[RB] = jnp.zeros((BLK, TOK), BF16)
    tab[...] = jnp.zeros(tab.shape, jnp.int32)
    for i in range(2, 6):
        loads[i].wait()
    ucnt, dcnt = ucnt_v[0], dcnt_v[0]
    io_u = lax.broadcasted_iota(jnp.int32, (RB, CB), 0)
    inv_u = jnp.full((RB, CB), KU, jnp.int32)
    for k in range(KU):
        live = ucnt > k
        target = urow_v[k]
        inv_u = jnp.where((io_u == target) & live, k, inv_u)
        tab[pl.ds(16 + k, 1), pl.ds(0, CB)] = jnp.where(live, target, RB)
    tab[pl.ds(0, RB), pl.ds(0, CB)] = inv_u
    io_d = lax.broadcasted_iota(jnp.int32, (CB, RB), 0)
    inv_d = jnp.full((CB, RB), KD, jnp.int32)
    for k in range(KD):
        live = dcnt > k
        target = drow_v[k]
        inv_d = jnp.where((io_d == target) & live, k, inv_d)
        tab[pl.ds(48 + k, 1), pl.ds(0, RB)] = jnp.where(live, target, CB)
    tab[pl.ds(24, CB), pl.ds(0, RB)] = inv_d
    tab_copy = pltpu.make_async_copy(tab, tab_s, lsem.at[15])
    tab_copy.start()

    for i in range(6, 15):
        loads[i].wait()

    def turn_down(j, carry):
        cols = pl.ds(al(j * BLK), BLK)
        for k in range(KD):
            dnr[k, :, cols] = dnr[k, :, cols].T
        return carry

    lax.fori_loop(0, RB, turn_down, 0)
    tab_copy.wait()

    for d in (1, 7, 2, 6, 3, 5, 4):
        g = mates[d]
        remote("x%d" % d, own.at[0], gat.at[0, g], mate(g, sec), recv=SEM["x0"] + g).wait_recv()

    lo, hi = pl.ds(0, 4), pl.ds(4, 4)
    send("g1a_m", gat.at[0, lo], gat.at[1, lo], y_m)
    send("g1a_p", gat.at[0, lo], gat.at[2, lo], y_p)
    send("g1b_p", gat.at[0, hi], gat.at[2, hi], y_p)
    send("g1b_m", gat.at[0, hi], gat.at[1, hi], y_m)

    def unpack(block, half):
        for i in range(2):
            a = gat[block, half * 4 + 2 * i].astype(F32)
            b = gat[block, half * 4 + 2 * i + 1].astype(F32)
            rows = pl.ds(START[block, half] + 16 * i, 16)
            xa[rows, :] = jnp.concatenate([a[:SHARE], b[:SHARE]], axis=0).astype(BF16)
            ga[rows, :] = jnp.concatenate([a[SHARE:], b[SHARE:]], axis=0).astype(BF16)

    def product(kind, rows, first):
        columns = []
        for u in range(QW // BLK):
            j = first + u
            if kind == 0:
                cols = pl.ds(al(j * BLK), BLK)
                blocks = [upr[tab_s[i, j], :, cols] for i in range(RB)]
            else:
                blocks = [dnr[tab_s[24 + j, i], :, pl.ds(i * BLK, BLK)] for i in range(RB)]
            columns.append(jnp.concatenate(blocks, axis=0))
        return dot_nn((xa, ga)[kind][rows, :], jnp.concatenate(columns, axis=1))

    quarter = [pl.ds(n * QW, QW) for n in range(2)]

    def forward(chunk, kind, then):
        t, m = chunk
        rows = pl.ds(t, m)
        for n in range(2):
            ss[kind, rows, quarter[n]] = product(kind, rows, (1 - core) * RB + n * (RB // 2)).astype(BF16)
            send("sib%d_%d_%d" % (t, kind, n), ss.at[kind, rows, quarter[n]], sr.at[kind, rows, quarter[n]], sibling)
        for n in range(2):
            hpo[kind, rows, quarter[n]] = product(kind, rows, core * RB + n * (RB // 2))
            arrived("sib%d_%d_%d" % (t, kind, n), sr.at[kind, rows, quarter[n]])
            if then is not None:
                combine(then, kind, n)

    def combine(chunk, kind, n):
        t, m = chunk
        rows = pl.ds(t, m)

        def body(i, carry):
            cols = pl.ds(al(n * QW + i * 256), 256)
            total = hpo[kind, rows, cols] + sr[kind, rows, cols].astype(F32)
            hpo[kind, rows, cols] = total
            qs[kind, rows, cols] = total.astype(BF16)
            return carry

        lax.fori_loop(0, QW // 256, body, 0)
        send("xlo%d_%d_%d" % (t, kind, n), qs.at[kind, rows, quarter[n]], qr.at[kind, rows, quarter[n]], across)

    def activate(chunk, n):
        t, m = chunk
        rows = pl.ds(t, m)
        for kind in range(2):
            arrived("xlo%d_%d_%d" % (t, kind, n), qr.at[kind, rows, quarter[n]])

        def body(i, carry):
            cols = pl.ds(al(n * QW + i * BLK), BLK)
            hidden = hpo[0, rows, cols] + qr[0, rows, cols].astype(F32)
            grad = hpo[1, rows, cols] + qr[1, rows, cols].astype(F32)
            act, slope = gelu_pair(hidden, grad)
            ah[core, 0, rows, cols] = act.astype(BF16)
            ah[core, 1, rows, cols] = slope.astype(BF16)
            return carry

        lax.fori_loop(0, QW // BLK, body, 0)
        send("act%d_%d" % (t, n), ah.at[core, :, rows, quarter[n]], ah.at[core, :, rows, quarter[n]], sibling)

    def met(chunk, n):
        t, m = chunk
        arrived("act%d_%d" % (t, n), ah.at[1 - core, :, pl.ds(t, m), quarter[n]])

    def term(rows, first, width, n):
        total = None
        for half in range(2):
            columns = []
            for u in range(RB // 2):
                i = n * (RB // 2) + u
                base = (half * HH + first) // BLK
                blocks = [upt[tab_s[i, j], :, pl.ds(j * BLK, BLK)] for j in range(base, base + width // BLK)]
                columns.append(jnp.concatenate(blocks, axis=0))
            part = dot_nn(ah[half, 1, rows, pl.ds(first, width)], jnp.concatenate(columns, axis=1))
            total = part if total is None else total + part
        return total

    def scatter(chunk, parts, n, part):
        t, m = chunk
        ip[n, pl.ds(t, m), :] = part.astype(BF16)
        for b, h in parts:
            span = pl.ds(32 * h, 32)
            if b == 0:
                rsr[0, n, span, :] = ip[n, pl.ds(START[b, h], 32), :]
            else:
                send(
                    "rs%d_%d_%d" % (b, h, n), ip.at[n, pl.ds(START[b, h], 32), :], rsr.at[b, n, span, :],
                    (None, y_p, y_m, y_2)[b],
                )

    def backward(chunk, parts):
        met(chunk, 0)
        met(chunk, 1)
        for n in range(2):
            scatter(chunk, parts, n, term(pl.ds(*chunk), 0, HH, n))

    unpack(0, 0)
    unpack(0, 1)
    forward(CA, 0, CA)
    forward(CA, 1, CA)
    arrived("g1a_m", gat.at[1, lo])
    send("g2_m", gat.at[1, lo], gat.at[3, lo], y_m)
    arrived("g1a_p", gat.at[2, lo])
    unpack(1, 0)
    unpack(2, 0)
    forward(CB1, 0, CB1)
    arrived("g1b_p", gat.at[2, hi])
    send("g2_p", gat.at[2, hi], gat.at[3, hi], y_p)
    forward(CB1, 1, CB1)
    arrived("g1b_m", gat.at[1, hi])
    unpack(1, 1)
    unpack(2, 1)

    upt[KU] = jnp.zeros((BLK, HW), BF16)

    def turn_up(j, carry):
        cols = pl.ds(al(j * BLK), BLK)
        for k in range(KU):
            upt[k, :, cols] = upr[k, :, cols].T
        return carry

    lax.fori_loop(0, CB, turn_up, 0)
    arrived("g2_m", gat.at[3, lo])
    arrived("g2_p", gat.at[3, hi])
    unpack(3, 0)
    unpack(3, 1)
    forward(CE, 0, CC)
    forward(CE, 1, CC)
    for n in range(2):
        combine(CD, 0, n)
        combine(CD, 1, n)
    for n in range(2):
        activate(CA, n)
    backward(CA, ((0, 0), (0, 1)))
    for n in range(2):
        activate(CB1, n)
    backward(CB1, ((1, 0), (2, 0)))

    def turn_x(i, carry):
        xt[i] = xa[:, pl.ds(al(i * BLK), BLK)].T
        return carry

    lax.fori_loop(0, RB, turn_x, 0)

    def turn_acts(first):
        for half in range(2):
            def turn_act(i, carry):
                block = ah[half, 0, pl.ds(first, 128), pl.ds(al(i * BLK), BLK)]
                act_t[half * RB + i, :, pl.ds(first, 128)] = block.T
                return carry

            lax.fori_loop(0, RB, turn_act, 0)

    turn_acts(0)
    for n in range(2):
        activate(CC, n)
    backward(CC, ((3, 0), (3, 1)))

    order = [lax.rem(me + d, 4) for d in range(4)]

    def finish(h):
        span = pl.ds(32 * h, 32)
        for b in range(1, 4):
            for n in range(2):
                arrived("rs%d_%d_%d" % (b, h, n), rsr.at[b, n, span, :])
        for i in range(2):
            rows = pl.ds(32 * h + 16 * i, 16)
            sums = []
            for n in range(2):
                total = rsr[0, n, rows, :].astype(F32)
                for b in range(1, 4):
                    total = total + rsr[b, n, rows, :].astype(F32)
                sums.append(total)
            for k in range(2):
                mine = [total[k * SHARE:(k + 1) * SHARE] for total in sums]
                xs[4 * h + 2 * i + k] = jnp.concatenate(mine, axis=0).astype(BF16)
        for k in (2, 1, 3, 0):
            g = order[k] + 4 * h
            send("f%d" % (4 * h + k), xs.at[g], xr.at[me], mate(g, before), recv=SEM["f0"] + me)

    def down_grad(step, carry):
        for u in range(3):
            j = step * 3 + u
            cols = pl.ds(al(j * BLK), BLK)
            picked = [act_t[tab_s[48 + k, j]] for k in range(KD)]
            dg_out[0, :, cols] = dot_nn(jnp.concatenate(picked, axis=0), ga[:, cols]).astype(BF16)
        return carry

    def up_grads(n):
        for half in range(2):
            def up_grad(step, carry):
                for u in range(3):
                    i = n * (RB // 2) + step * 3 + u
                    j = half * RB + i
                    weights = ah[half, 1, :, pl.ds(al(i * BLK), BLK)]
                    picked = [xt[tab_s[16 + k, j]] for k in range(KU)]
                    ug_out[0, :, pl.ds(al(j * BLK), BLK)] = dot_nn(jnp.concatenate(picked, axis=0), weights).astype(BF16)
                return carry

            lax.fori_loop(0, RB // 6, up_grad, 0)

    span = pl.ds(*CD)
    activate(CD, 0)
    finish(0)
    met(CD, 0)
    for n in range(2):
        acc[n] = term(span, 0, QW, n)
    activate(CD, 1)
    up_grads(0)
    met(CD, 1)
    for n in range(2):
        scatter(CD, ((1, 1), (2, 1)), n, acc[n] + term(span, QW, QW, n))
    turn_acts(128)
    lax.fori_loop(0, RB // 6, down_grad, 0)
    finish(1)
    lax.fori_loop(RB // 6, RB // 3, down_grad, 0)
    up_grads(1)

    for g in range(8):
        arrived_f(g)
    arrived("zg", zown)
    keep = sec < n_sec - 1
    for r in range(4):
        base = zown[r].astype(F32)[SHARE:]
        base = jnp.concatenate([base[:, :TW // 2], base[:, TW // 2:]], axis=0)
        first = (r % 2) * 4 + r // 2
        v = (base + (xr[first].astype(F32) + xr[first + 2].astype(F32)))
        v = jnp.where(keep, v, 0.0)
        recv_out[0, :, r * TW:(r + 1) * TW] = jnp.concatenate([v[:SHARE], v[SHARE:]], axis=1).astype(BF16)
    for copy in sent:
        copy.wait_send()


def shards(layer_input, output_grad, up_panels, up_rows, up_counts, down_panels, down_rows, down_counts):
    hbm = pl.BlockSpec(memory_space=pl.ANY)
    vmem = pltpu.VMEM
    return pl.pallas_call(
        kernel,
        out_shape=(
            vmem((1, SHARE, D), BF16), vmem((1, KU * BLK, HW), BF16), vmem((1, KD * BLK, TW), BF16),
        ),
        in_specs=[hbm] * 8,
        out_specs=(pl.BlockSpec(memory_space=pltpu.VMEM),) * 3,
        scratch_shapes=[
            vmem((1, SHARE, D), BF16), vmem((1, SHARE, D), BF16),
            vmem((KU, 1, CB), jnp.int32), vmem((1, 1, CB), jnp.int32),
            vmem((KD, 1, RB), jnp.int32), vmem((1, 1, RB), jnp.int32),
            vmem((64, 128), jnp.int32), pltpu.SMEM((64, 128), jnp.int32),
            vmem((4, 2 * SHARE, TW), BF16), vmem((4, 2 * SHARE, TW), BF16),
            vmem((4, 8, 2 * SHARE, TW), BF16),
            vmem((TOK, TW), BF16), vmem((TOK, TW), BF16),
            vmem((RB + 1, BLK, TOK), BF16),
            vmem((KU + 1, BLK, HW), BF16), vmem((KD + 1, BLK, TW), BF16),
            vmem((KU + 1, BLK, HW), BF16),
            vmem((2, TOK, HH), F32),
            vmem((2, TOK, HH), BF16), vmem((2, TOK, HH), BF16),
            vmem((2, TOK, HH), BF16), vmem((2, TOK, HH), BF16),
            vmem((2, 2, TOK, HH), BF16),
            vmem((CB + 1, BLK, TOK), BF16),
            vmem((2, TOK, TW // 2), BF16), vmem((2, 64, TW // 2), F32), vmem((4, 2, 64, TW // 2), BF16),
            vmem((8, 2 * SHARE, TW // 2), BF16), vmem((8, 2 * SHARE, TW // 2), BF16),
            pltpu.SemaphoreType.DMA((16,)),
            pltpu.SemaphoreType.DMA((len(NAMES),)),
            pltpu.SemaphoreType.DMA((len(NAMES),)),
        ],
        compiler_params=pltpu.CompilerParams(
            collective_id=0, has_side_effects=True, vmem_limit_bytes=50 * 1024 * 1024
        ),
    )(
        layer_input, output_grad, up_panels, jnp.swapaxes(up_rows, 0, 1), up_counts,
        down_panels, jnp.swapaxes(down_rows, 0, 1), down_counts,
    )


def solution(mesh):
    in_specs = (
        P("section", ("row", "col"), None),
        P("section", ("row", "col"), None),
        P("section", "row", "col"),
        P("section", "row", "col"),
        P("section", "row", "col"),
        P("section", "col", "row"),
        P("section", "col", "row"),
        P("section", "col", "row"),
    )
    out_specs = (
        P("section", ("row", "col"), None),
        P("section", "row", "col"),
        P("section", "col", "row"),
    )
    return jax.shard_map(shards, mesh=mesh, in_specs=in_specs, out_specs=out_specs, check_vma=False)
```

time: 79.9 us -> 75 us (0.939)
  Pallas kernels: 75.1 us -> 70.8 us
    pallas_call x1, Pallas kernels: 75.1 us -> 70.8 us  [shards(): pl.pallas_call(kernel, out_shape=(vmem((1, SHARE, D), BF16), vmem((1, KU...]
where the time goes in v3:
time: 75 us; the launch traced here: 74.9 us
  Pallas kernels  70.8 us (94%)
  local copies, waits for them, and re-layouts  3.45 us (5%)
    pallas_call x1, Pallas kernels, shards(): pl.pallas_call(kernel, out_shape=(vmem((1, SHARE, D), BF16), vmem((1, KU...  70.8 us
    unnamed x3, local copies, waits for them, and re-layouts  3.45 us

profile of v3, /device:TPU:1, one launch (start us, length us, event | category | flops | bytes accessed | tf_op | source)
XLA Modules:
  0.0 74.9 jit_solution(7038329715897787279)
XLA Ops:
  0.6 70.8 %shard_map.103 = (bf16[1,8,6144]{2,1,0:T(8,128)(2,1)S(1)}, bf16[1,384,3072]{2,1,0:T(8,128)(2,1)S(1)}, bf16[1,768,1536]{2,1,0:T(8,128)(2,1)S(1)}) custom-call(bf16[1,8,6144]{2,1,0:T(8,128)(2,1)} %x_hbm.1, bf16[1,8,6144]{2,1,0:T(8,128)(2,1)} %g_hbm.1, bf16[1,384,3072]{2,1,0:T(8,128)(2,1)} %up_hbm.1, s32[3,1,24]{2,1,0:T(1,128)} %bitcast.3, ...), custom_call_target="tpu_custom_call" | custom-call | tf_op jit(solution)/shard_map/pallas_call | solution.py:448
  71.4 0.6 copy.14
  72.1 1.4 %copy.15 = bf16[1,384,3072]{2,1,0:T(8,128)(2,1)} copy(bf16[1,384,3072]{2,1,0:T(8,128)(2,1)S(1)} %get-tuple-element.4) | data formatting | bytes 4718592
  73.5 1.4 %copy.16 = bf16[1,768,1536]{2,1,0:T(8,128)(2,1)} copy(bf16[1,768,1536]{2,1,0:T(8,128)(2,1)S(1)} %get-tuple-element.5) | data formatting | bytes 4718592

commit v4 on v3

--- a/solution.py
+++ b/solution.py
@@ -148,10 +148,10 @@
 
     pl.semaphore_wait(barrier, 18)
 
-    for d in (1, 7, 2, 6, 3, 5, 4):
-        g = mates[d]
+    x = lax.rem(me, 4)
+    for d, (dx, dc) in enumerate(((2, 0), (2, 1), (1, 0), (3, 0), (1, 1), (3, 1), (0, 1))):
+        g = lax.rem(core + dc, 2) * 4 + lax.rem(x + dx, 4)
         send("x%d" % d, own.at[mate_row(g)], gat.at[0, me], mate(g, sec), recv=SEM["x0"] + me)
-    send("zg", own, zown, mate(me, before))
     gat[0, me] = own[row]
 
     upr[KU] = jnp.zeros((BLK, HW), BF16)
@@ -203,6 +203,8 @@
     send("g1b_p", gat.at[0, hi], gat.at[2, hi], y_p)
     send("g1b_m", gat.at[0, hi], gat.at[1, hi], y_m)
 
+    send("zg", own, zown, mate(me, before))
+
     def unpack(block, half):
         for i in range(2):
             a = gat[block, half * 4 + 2 * i].astype(F32)
@@ -353,16 +355,17 @@
 
     lax.fori_loop(0, RB, turn_x, 0)
 
-    def turn_acts(first):
+    def turn_acts(first, n):
         for half in range(2):
             def turn_act(i, carry):
                 block = ah[half, 0, pl.ds(first, 128), pl.ds(al(i * BLK), BLK)]
                 act_t[half * RB + i, :, pl.ds(first, 128)] = block.T
                 return carry
 
-            lax.fori_loop(0, RB, turn_act, 0)
-
-    turn_acts(0)
+            lax.fori_loop(n * (RB // 2), (n + 1) * (RB // 2), turn_act, 0)
+
+    turn_acts(0, 0)
+    turn_acts(0, 1)
     for n in range(2):
         activate(CC, n)
     backward(CC, ((3, 0), (3, 1)))
@@ -412,16 +415,17 @@
 
     span = pl.ds(*CD)
     activate(CD, 0)
-    finish(0)
     met(CD, 0)
     for n in range(2):
         acc[n] = term(span, 0, QW, n)
+    turn_acts(128, 0)
     activate(CD, 1)
     up_grads(0)
     met(CD, 1)
     for n in range(2):
         scatter(CD, ((1, 1), (2, 1)), n, acc[n] + term(span, QW, QW, n))
-    turn_acts(128)
+    turn_acts(128, 1)
+    finish(0)
     lax.fori_loop(0, RB // 6, down_grad, 0)
     finish(1)
     lax.fori_loop(RB // 6, RB // 3, down_grad, 0)

time: 75 us -> 71.4 us (0.952)
  Pallas kernels: 70.8 us -> 67.3 us
    pallas_call x1, Pallas kernels: 70.8 us -> 67.3 us  [shards(): pl.pallas_call(kernel, out_shape=(vmem((1, SHARE, D), BF16), vmem((1, KU...]
where the time goes in v4:
time: 71.4 us
  Pallas kernels  67.3 us (94%)
  local copies, waits for them, and re-layouts  3.45 us (5%)
    pallas_call x1, Pallas kernels, shards(): pl.pallas_call(kernel, out_shape=(vmem((1, SHARE, D), BF16), vmem((1, KU...  67.3 us
    unnamed x3, local copies, waits for them, and re-layouts  3.45 us

profile of v4, /device:TPU:1, one launch (start us, length us, event | category | flops | bytes accessed | tf_op | source)
XLA Modules:
  0.0 71.4 jit_solution(17501996388502931733)
XLA Ops:
  0.6 67.3 %shard_map.103 = (bf16[1,8,6144]{2,1,0:T(8,128)(2,1)S(1)}, bf16[1,384,3072]{2,1,0:T(8,128)(2,1)S(1)}, bf16[1,768,1536]{2,1,0:T(8,128)(2,1)S(1)}) custom-call(bf16[1,8,6144]{2,1,0:T(8,128)(2,1)} %x_hbm.1, bf16[1,8,6144]{2,1,0:T(8,128)(2,1)} %g_hbm.1, bf16[1,384,3072]{2,1,0:T(8,128)(2,1)} %up_hbm.1, s32[3,1,24]{2,1,0:T(1,128)} %bitcast.3, ...), custom_call_target="tpu_custom_call" | custom-call | tf_op jit(solution)/shard_map/pallas_call | solution.py:452
  67.9 0.6 copy.14
  68.6 1.4 %copy.15 = bf16[1,384,3072]{2,1,0:T(8,128)(2,1)} copy(bf16[1,384,3072]{2,1,0:T(8,128)(2,1)S(1)} %get-tuple-element.4) | data formatting | bytes 4718592
  70.0 1.4 %copy.16 = bf16[1,768,1536]{2,1,0:T(8,128)(2,1)} copy(bf16[1,768,1536]{2,1,0:T(8,128)(2,1)S(1)} %get-tuple-element.5) | data formatting | bytes 4718592

commit v5 on v4

--- a/solution.py
+++ b/solution.py
@@ -425,8 +425,8 @@
     for n in range(2):
         scatter(CD, ((1, 1), (2, 1)), n, acc[n] + term(span, QW, QW, n))
     turn_acts(128, 1)
+    lax.fori_loop(0, RB // 6, down_grad, 0)
     finish(0)
-    lax.fori_loop(0, RB // 6, down_grad, 0)
     finish(1)
     lax.fori_loop(RB // 6, RB // 3, down_grad, 0)
     up_grads(1)

time: 71.4 us -> 71.6 us (level)
  no operation moved by 1% of the time
where the time goes in v5:
time: 71.6 us; the launch traced here: 71.5 us
  Pallas kernels  67.4 us (94%)
  local copies, waits for them, and re-layouts  3.45 us (5%)
    pallas_call x1, Pallas kernels, shards(): pl.pallas_call(kernel, out_shape=(vmem((1, SHARE, D), BF16), vmem((1, KU...  67.4 us
    unnamed x3, local copies, waits for them, and re-layouts  3.45 us

profile of v5, /device:TPU:1, one launch (start us, length us, event | category | flops | bytes accessed | tf_op | source)
XLA Modules:
  0.0 71.5 jit_solution(18346638691502277219)
XLA Ops:
  0.6 67.4 %shard_map.103 = (bf16[1,8,6144]{2,1,0:T(8,128)(2,1)S(1)}, bf16[1,384,3072]{2,1,0:T(8,128)(2,1)S(1)}, bf16[1,768,1536]{2,1,0:T(8,128)(2,1)S(1)}) custom-call(bf16[1,8,6144]{2,1,0:T(8,128)(2,1)} %x_hbm.1, bf16[1,8,6144]{2,1,0:T(8,128)(2,1)} %g_hbm.1, bf16[1,384,3072]{2,1,0:T(8,128)(2,1)} %up_hbm.1, s32[3,1,24]{2,1,0:T(1,128)} %bitcast.3, ...), custom_call_target="tpu_custom_call" | custom-call | tf_op jit(solution)/shard_map/pallas_call | solution.py:452
  68.0 0.6 copy.14
  68.7 1.4 %copy.15 = bf16[1,384,3072]{2,1,0:T(8,128)(2,1)} copy(bf16[1,384,3072]{2,1,0:T(8,128)(2,1)S(1)} %get-tuple-element.4) | data formatting | bytes 4718592
  70.1 1.4 %copy.16 = bf16[1,768,1536]{2,1,0:T(8,128)(2,1)} copy(bf16[1,768,1536]{2,1,0:T(8,128)(2,1)S(1)} %get-tuple-element.5) | data formatting | bytes 4718592
